TPU v7x, 512 devices: a whole 4x8x8 slice. The times are simulated.
512 devices in a mesh: row: 16 (over y_hi, x), col: 16 (over z, core), day: 2 (over y_lo).
Axes of the slice: x: 4, y: 8 (y_hi: 4, y_lo: 2; y = y_hi * 2 + y_lo), z: 8, core: 2. Of those that a mesh axis runs over, the one named last changes fastest.
Arguments:
- spectra: bfloat16 [2, 6, 1024, 512], P('day', None, ('row', 'col')), may hold values from -180 to 180
- avail: int32 [2, 6, 1024], P('day', None, ('row', 'col')), may hold values 0 or 1
Outputs:
- pws: bfloat16 [16, 16, 32, 64, 128], P('row', 'col', None, 'day')
All inputs are finite; a program needn't handle non-finite values. No bound on the sum of `avail` on one device may be relied on, other than what follows from the above.
Results may differ from a plain program's by a relative error of at most 0.018.
Values may be sent and summed in bfloat16 or wider, within the bound.
No kernel may reach another device: no remote copies, remote signals or barrier semaphores. Data moves between devices by JAX's collectives and lax.ppermute only.
A program may use at most 64 MiB of HBM per device.

v0:
```python
import math

import jax
import jax.numpy as jnp
from jax import lax
from jax.sharding import PartitionSpec as P

LAGS = 128


def spread_2(value, axis, source):
    kept = jnp.where(lax.axis_index(axis) == source, value, 0).astype(value.dtype)
    return lax.psum(kept, axis)


def whiten(spectra, avail):
    values = spectra.astype(jnp.float32)
    bins = values.shape[-1] // 2
    power = values[..., :bins] ** 2 + values[..., bins:] ** 2
    level = jnp.mean(power, axis=-1, keepdims=True) + 1e-06
    factor = avail.astype(jnp.float32)[..., None] / jnp.sqrt(power + 0.09 * level)
    return (values * jnp.concatenate([factor, factor], axis=-1)).astype(jnp.bfloat16)


def lag_table(bins, lags, hours):
    freq = (jnp.arange(bins, dtype=jnp.float32) + 0.5) * (math.pi / bins)
    shifts = jnp.arange(lags, dtype=jnp.float32) - lags // 2
    angles = freq[:, None] * shifts[None, :]
    cosine = jnp.cos(angles)
    sine = jnp.sin(angles)
    upper = jnp.concatenate([cosine, sine], axis=1)
    lower = jnp.concatenate([-sine, cosine], axis=1)
    table = jnp.concatenate([upper, lower], axis=0) * (1.0 / math.sqrt(hours * bins))
    return table.astype(jnp.bfloat16)


def cross_spectrum(first, second):
    bins = first.shape[-1] // 2
    first_re, first_im = (first[..., :bins], first[..., bins:])
    second_re, second_im = (second[..., :bins], second[..., bins:])
    real_sum = jnp.einsum("hik,hjk->ijk", first_re, second_re, preferred_element_type=jnp.float32)
    real_sum = real_sum + jnp.einsum(
        "hik,hjk->ijk", first_im, second_im, preferred_element_type=jnp.float32
    )
    imag_sum = jnp.einsum("hik,hjk->ijk", first_im, second_re, preferred_element_type=jnp.float32)
    imag_sum = imag_sum - jnp.einsum(
        "hik,hjk->ijk", first_re, second_im, preferred_element_type=jnp.float32
    )
    return jnp.concatenate([real_sum, imag_sum], axis=-1).astype(jnp.bfloat16)


def mix_diagonal(cross, extra, same):
    half = extra.shape[0]
    bins = extra.shape[-1] // 2
    flipped = jnp.concatenate([extra[..., :bins], -extra[..., bins:]], axis=-1)
    rows_idx = jnp.arange(half, dtype=jnp.int32)[:, None, None]
    cols_idx = jnp.arange(half, dtype=jnp.int32)[None, :, None]
    left = cross[:, :half]
    zeros = jnp.zeros_like(left)
    left = jnp.where(rows_idx < cols_idx, left, jnp.where(rows_idx > cols_idx, flipped, zeros))
    mixed = jnp.concatenate([left, cross[:, half:]], axis=1)
    return jnp.where(same, mixed, cross)


def body(spectra, avail):
    day_count, hour_count, local_count, width = spectra.shape
    bins = width // 2
    white = whiten(spectra, avail)
    row_side = lax.all_gather(white, "col", axis=2, tiled=True)
    col_side = spread_2(row_side, "row", lax.axis_index("col"))
    row_id = lax.axis_index("row")
    col_id = lax.axis_index("col")
    block_size = row_side.shape[2]
    half = block_size // 2
    below = row_id > col_id
    same = row_id == col_id
    firsts = jnp.where(below, col_side[:, :, half:], row_side[:, :, :half])
    seconds = jnp.where(below, row_side, col_side)
    bottoms = row_side[:, :, half:]
    table = lag_table(bins, LAGS, hour_count)
    cross = cross_spectrum(firsts[0], seconds[0])
    extra = cross_spectrum(bottoms[0], bottoms[0])
    cross = mix_diagonal(cross, extra, same)
    both = jnp.dot(
        cross.reshape(half * block_size, width), table, preferred_element_type=jnp.float32
    )
    both = both.reshape(half, block_size, 2 * LAGS)
    corr = both[..., :LAGS]
    hilb = both[..., LAGS:]
    amp = corr * corr + hilb * hilb
    spread = jnp.mean(amp, axis=-1, keepdims=True) + 1e-06
    inverse = 1.0 / jnp.sqrt(amp + 0.01 * spread)
    phase_sum = both * jnp.concatenate([inverse, inverse], axis=-1)
    lin_total, phase_total = (
        lax.psum_scatter(corr.astype(jnp.bfloat16), "day", scatter_dimension=1, tiled=True).astype(
            jnp.float32
        ),
        lax.psum_scatter(
            phase_sum.astype(jnp.bfloat16), "day", scatter_dimension=1, tiled=True
        ).astype(jnp.float32),
    )
    total_days = day_count * lax.axis_size("day")
    coherence = phase_total[..., :LAGS] ** 2 + phase_total[..., LAGS:] ** 2
    result = (lin_total * coherence / float(total_days * total_days)).astype(jnp.bfloat16)
    return result[None, None]


def solution(mesh):
    placed = (P("day", None, ("row", "col"), None), P("day", None, ("row", "col")))
    return jax.shard_map(
        body,
        mesh=mesh,
        in_specs=placed,
        out_specs=P("row", "col", None, "day", None),
        check_vma=False,
    )
```

profile of v0, /device:TPU:1, one launch (start us, length us, event | category | flops | bytes accessed | tf_op | source)
XLA Modules:
  0.0 290.6 jit_solution(12163087068897903145)
XLA Ops:
  6.5 0.0 all-reduce.2.cloned.1.call-start
  6.5 0.7 copy_convert_fusion
  7.3 0.1 fusion.41
  7.4 0.7 convert_bitcast_fusion
  8.1 0.1 rsqrt_multiply_fusion
  8.2 0.8 fusion.38
  8.9 25.9 %all_gather.3 = bf16[1,6,64,512]{3,1,0,2:T(8,128)(2,1)S(1)} all-gather(bf16[1,6,4,512]{3,1,0,2:T(8,128)(2,1)S(1)} %fusion.38), channel_id=1, replica_groups=mesh['row'=16,'col'=16,'day'=2] {'col'}, dimensions={2}, use_global_device_ids=true | all-gather | bytes 417792 | tf_op jit(solution)/shard_map/all_gather | solution.py:69
  34.8 1.1 copy.30
  35.9 1.1 broadcast_select_fusion
  37.1 0.0 all-reduce.2.cloned.1.call-update
  37.1 0.0 reduce-scatter.5.cloned.1.call-start
  37.2 0.5 multiply_sine_fusion
  37.7 160.1 %all-reduce.2.cloned.1.call-done = bf16[1,6,64,512]{2,1,3,0:T(8,128)(2,1)} async-done(((bf16[1,6,64,512]{2,1,3,0:T(8,128)(2,1)}), bf16[1,6,64,512]{2,1,3,0:T(8,128)(2,1)}) %all-reduce.2.cloned.1.call-update) | async-done | bytes 393232 | tf_op jit(solution)/shard_map/psum | solution.py:13
  197.8 1.9 slice_bitcast_fusion
  200.0 0.8 fusion.27
  200.8 0.0 copy-start
  200.8 0.8 fusion.23
  201.6 0.5 copy-done
  202.0 0.1 broadcast_select_fusion.1
  202.1 0.8 fusion.13
  202.9 0.8 fusion.16
  203.7 0.9 fusion.9
  204.5 1.0 negate_bitcast_fusion
  205.5 0.8 fusion.7
  206.4 0.9 fusion.8
  207.2 4.5 %fusion.1 = (bf16[32,32,512]{1,0,2:T(8,128)(2,1)S(1)}, bf16[32,32,512]{1,0,2:T(8,128)(2,1)S(1)}) fusion(bf16[32,64,256]{1,0,2:T(8,128)(2,1)S(1)} %fusion.7, bf16[32,64,256]{1,0,2:T(8,128)(2,1)S(1)} %fusion.8, bf16[32,32,256]{1,0,2:T(8,128)(2,1)S(1)} %negate_bitcast_fusion, bf16[32,32,256]{1,0,2:T(8,128)(2,1)S(1)} %fusion.9, ...), kind=kLoop, calls=%fused_computation.6 | loop fusion | flops 2621440 | bytes 5244928 | tf_op jit(solution)/shard_map/jit(_where)/select_n | solution.py:60
  211.7 3.2 %fusion.3 = bf16[32,64,512]{1,0,2:T(8,128)(2,1)S(1)} fusion(bf16[32,64,256]{1,0,2:T(8,128)(2,1)S(1)} %fusion.8, bf16[32,64,256]{1,0,2:T(8,128)(2,1)S(1)} %fusion.7, bf16[32,32,512]{1,0,2:T(8,128)(2,1)S(1)} %get-tuple-element.6, bf16[32,32,512]{1,0,2:T(8,128)(2,1)S(1)} %get-tuple-element.5, pred[]{:T(512)S(6)} %eq.4), kind=kLoop, calls=%fused_computation.8 | loop fusion | flops 9437184 | bytes 6291457 | tf_op jit(solution)/shard_map/jit(_where)/select_n | solution.py:62
  214.9 2.5 fusion.4
  217.3 0.3 fusion.37
  217.7 0.3 add_rsqrt_fusion
  218.1 1.4 fusion.6
  219.5 0.0 reduce-scatter.5.cloned.1.call-update
  219.5 0.0 reduce-scatter.3.cloned.1.call-start
  219.5 0.9 slice.167
  220.4 0.0 reduce-scatter.3.cloned.1.call-update
  220.4 36.2 %reduce-scatter.5.cloned.1.call-done = bf16[32,32,256]{2,1,0:T(8,128)(2,1)} async-done(((bf16[32,64,256]{2,1,0:T(8,128)(2,1)}), bf16[32,32,256]{2,1,0:T(8,128)(2,1)}) %reduce-scatter.5.cloned.1.call-update) | async-done | bytes 524304 | tf_op jit(solution)/shard_map/reduce_scatter | solution.py:98
  256.7 1.1 convert_element_type.40
  257.8 24.5 %reduce-scatter.3.cloned.1.call-done = bf16[32,32,128]{2,1,0:T(8,128)(2,1)} async-done(((bf16[32,64,128]{2,1,0:T(8,128)(2,1)}), bf16[32,32,128]{2,1,0:T(8,128)(2,1)}) %reduce-scatter.3.cloned.1.call-update) | async-done | bytes 262160 | tf_op jit(solution)/shard_map/reduce_scatter | solution.py:95
  282.3 1.8 fusion.35
  (13 shorter events, 0.3 us)
Async XLA Ops:
  6.5 191.3 %all-reduce.2.cloned.1.call-start = ((), (), s32[]{:S(2)}) async-start(), calls=%async_computation.2 | async-start | bytes 2097152 | tf_op jit(solution)/shard_map/psum | solution.py:13
  37.1 219.6 %reduce-scatter.5.cloned.1.call-start = ((), (), s32[]{:S(2)}) async-start(), calls=%async_computation.4 | async-start | bytes 1572864 | tf_op jit(solution)/shard_map/reduce_scatter | solution.py:98
  200.8 1.2 copy-start
  219.5 62.9 %reduce-scatter.3.cloned.1.call-start = ((), (), s32[]{:S(2)}) async-start(), calls=%async_computation.3 | async-start | bytes 786432 | tf_op jit(solution)/shard_map/reduce_scatter | solution.py:95
Sparse Core Ops, SparseCore 0:
  37.2 160.5 all-reduce.1
  219.6 37.0 reduce-scatter.4
  259.5 22.8 reduce-scatter.2
where the time goes:
time: 291 us
  waiting for transfers between devices  221 us (76%)
  blocking collectives  25.9 us (9%)
  other arithmetic  18.7 us (6%)
  between operations  13.3 us (5%)
  matrix products  8.99 us (3%)
    psum x1, waiting for transfers between devices, spread_2(): return lax.psum(kept, axis)  160 us
    reduce_scatter x1, waiting for transfers between devices, body(): lax.psum_scatter(phase_sum.astype(jnp.bfloat16), 'day', scatter_dimension...  36.2 us
    all_gather x1, blocking collectives, body(): row_side = lax.all_gather(white, 'col', axis=2, tiled=True)  25.9 us
    reduce_scatter x1, waiting for transfers between devices, body(): lax.psum_scatter(corr.astype(jnp.bfloat16), 'day', scatter_dimension=1, t...  24.5 us
  transfers between devices with their start and end apart: 3, of which 3 were waited for; matrix products, arithmetic and copies ran while one was open for 1% of the time, Pallas kernels for 0%

commit v1 on v0

v1 whole, which is shorter than its diff:
```python
import math

import jax
import jax.numpy as jnp
import ml_dtypes
import numpy as np
from jax import lax
from jax.experimental import pallas as pl
from jax.experimental.pallas import tpu as pltpu
from jax.sharding import PartitionSpec as P

BINS = 256
LAGS = 128
HOURS = 6
AXES = ("row", "col", "day")


def lag_table():
    freq = (np.arange(BINS) + 0.5) * (math.pi / BINS)
    angles = freq[:, None] * (np.arange(LAGS) - LAGS // 2)[None, :]
    upper = np.concatenate([np.cos(angles), np.sin(angles)], 1)
    lower = np.concatenate([-np.sin(angles), np.cos(angles)], 1)
    return (np.concatenate([upper, lower], 0) / math.sqrt(HOURS * BINS)).astype(ml_dtypes.bfloat16)

def whiten_kernel(spec_ref, avail_ref, out_ref, rows):
    eye = lax.broadcasted_iota(jnp.int32, (4, 4), 0) == lax.broadcasted_iota(jnp.int32, (4, 4), 1)
    avail = avail_ref[0].astype(jnp.float32)
    for h in range(HOURS):
        x = spec_ref[0, h].astype(jnp.float32)
        re, im = x[:, :BINS], x[:, BINS:]
        power = re * re + im * im
        level = jnp.mean(power, axis=1, keepdims=True) + 1e-06
        usable = jnp.sum(jnp.where(eye, avail[h:h + 1, :], 0.0), axis=1, keepdims=True)
        factor = usable * lax.rsqrt(power + 0.09 * level)
        white = (re * factor, im * factor)
        for part in range(4):
            piece = white[part // 2][:, (part % 2) * 128:(part % 2) * 128 + 128]
            rows[pl.ds(part * 24 + h, 4, stride=6), :] = piece
    out_ref[...] = rows[...].astype(jnp.bfloat16)

def whiten(spectra, avail):
    return pl.pallas_call(
        whiten_kernel,
        out_shape=jax.ShapeDtypeStruct((96, 128), jnp.bfloat16),
        scratch_shapes=[pltpu.VMEM((96, 128), jnp.float32)],
        name="whiten",
    )(spectra, avail)

def stack_kernel(place_ref, row_ref, col_ref, table_ref, out_ref, rows, firsts, seconds, cross, both):
    row_id = place_ref[0]
    col_id = place_ref[1]
    day_id = place_ref[2]
    below = row_id > col_id
    same = row_id == col_id
    corner = jnp.logical_and(same, day_id == 0)
    step = pl.program_id(0)

    def spread_first(day, j, block, slot):
        v = block.astype(jnp.float32)
        for part in range(4):
            firsts[slot, part, pl.ds(pl.multiple_of(day * 192 + j * 24, 8), 24), :] = v[part * 24:part * 24 + 24]

    def spread_second(day, j, block):
        v = block.astype(jnp.float32)
        for part in range(4):
            rows[part, pl.ds(pl.multiple_of(day * 192 + j * 24, 8), 24), :] = v[part * 24:part * 24 + 24]

    def split_hours(slot):
        for day in range(2):
            for h in range(HOURS):
                for part in range(4):
                    v = rows[part, pl.ds(day * 192 + h, 32, stride=6), :]
                    if slot == 1 and part >= 2:
                        v = -v
                    seconds[slot, day, h, part] = v

    @pl.when(step == 0)
    def _():
        for day in range(2):
            @pl.loop(0, 8)
            def _(j):
                @pl.when(below)
                def _():
                    spread_first(day, j, col_ref[j + 8, day], 0)
                    spread_second(day, j, row_ref[j + 8 * day_id, day])
                @pl.when(jnp.logical_not(below))
                def _():
                    spread_first(day, j, row_ref[j, day], 0)
                    @pl.when(same)
                    def _():
                        spread_second(day, j, row_ref[j + 8 * day_id, day])
                    @pl.when(jnp.logical_not(same))
                    def _():
                        spread_second(day, j, col_ref[j + 8 * day_id, day])
        split_hours(0)
        @pl.when(corner)
        def _():
            for day in range(2):
                @pl.loop(0, 8)
                def _(j):
                    v = row_ref[j + 8, day]
                    spread_second(day, j, v)
                    w = v.astype(jnp.float32)
                    for part in range(4):
                        piece = w[part * 24:part * 24 + 24]
                        firsts[1, part, pl.ds(pl.multiple_of(day * 192 + j * 24, 8), 24), :] = piece if part < 2 else -piece
            split_hours(1)

    def tile(src, day, a, q):
        acc = [None] * 4
        for h in range(HOURS):
            first = [firsts[src, part, pl.ds(day * 192 + a * 6 + h, 1), :] for part in range(4)]
            second = [seconds[src, day, h, part, pl.ds(q * 8, 8), :] for part in range(4)]
            for k in range(2):
                fr, fi = first[k], first[k + 2]
                sr, si = second[k], second[k + 2]
                re = fr * sr + fi * si
                im = fi * sr - fr * si
                acc[k] = re if h == 0 else acc[k] + re
                acc[k + 2] = im if h == 0 else acc[k + 2] + im
        return jnp.concatenate(acc, axis=1)

    @pl.loop(0, 8)
    def _(i):
        a = step * 8 + i
        for day in range(2):
            tiles = []
            for q in range(4):
                src = jnp.where(jnp.logical_and(corner, q < step), 1, 0)
                tiles.append(tile(src, day, a, q))
            cross[day, pl.ds(pl.multiple_of(i * 32, 32), 32), :] = jnp.concatenate(tiles, axis=0).astype(jnp.bfloat16)

    @pl.when(corner)
    def _():
        @pl.loop(0, 8)
        def _(i):
            a = step * 8 + i
            j = lax.broadcasted_iota(jnp.int32, (32, 512), 0)
            for day in range(2):
                other = tile(1, day, a, step)
                other = jnp.concatenate([other] * 4, axis=0)
                at = pl.ds(pl.multiple_of(i * 32, 32), 32)
                own = cross[day, at, :].astype(jnp.float32)
                inside = jnp.logical_and(j // 8 == step, j < a)
                own = jnp.where(inside, other, jnp.where(j == a, 0.0, own))
                cross[day, at, :] = own.astype(jnp.bfloat16)

    for day in range(2):
        both[day] = jnp.dot(cross[day], table_ref[...], preferred_element_type=jnp.float32)

    @pl.loop(0, 8)
    def _(i):
        at = pl.ds(pl.multiple_of(i * 32, 32), 32)
        lin = pr = pi = None
        for day in range(2):
            corr = both[day, at, :LAGS]
            hilb = both[day, at, LAGS:]
            amp = corr * corr + hilb * hilb
            spread = jnp.mean(amp, axis=1, keepdims=True) + 1e-06
            inverse = lax.rsqrt(amp + 0.01 * spread)
            if day == 0:
                lin, pr, pi = corr, corr * inverse, hilb * inverse
            else:
                lin, pr, pi = lin + corr, pr + corr * inverse, pi + hilb * inverse
        out_ref[i] = (lin * (pr * pr + pi * pi) * 0.25).astype(jnp.bfloat16)

def stack(place, row_side, col_side):
    table = jnp.asarray(lag_table())
    whole = lambda n: (lambda i: (0,) * n)
    return pl.pallas_call(
        stack_kernel,
        grid=(4,),
        in_specs=[
            pl.BlockSpec(memory_space=pltpu.SMEM),
            pl.BlockSpec((16, 2, 96, 128), whole(4)),
            pl.BlockSpec((16, 2, 96, 128), whole(4)),
            pl.BlockSpec((512, 256), whole(2)),
        ],
        out_specs=pl.BlockSpec((8, 32, 128), lambda i: (i, 0, 0)),
        out_shape=jax.ShapeDtypeStruct((32, 32, 128), jnp.bfloat16),
        scratch_shapes=[
            pltpu.VMEM((4, 384, 128), jnp.float32),
            pltpu.VMEM((2, 4, 384, 128), jnp.float32),
            pltpu.VMEM((2, 2, 6, 4, 32, 128), jnp.float32),
            pltpu.VMEM((2, 256, 512), jnp.bfloat16),
            pltpu.VMEM((2, 256, 256), jnp.float32),
        ],
        compiler_params=pltpu.CompilerParams(vmem_limit_bytes=32 * 1024 * 1024),
        name="stack",
    )(place, row_side, col_side, table)

def body(spectra, avail):
    n_row, n_col, n_day = (lax.axis_size(name) for name in AXES)
    place = jnp.stack([lax.axis_index(name) for name in AXES]).astype(jnp.int32)
    white = whiten(spectra, avail)
    pair = lax.all_gather(white, "day", axis=0)
    turn = [
        ((r * n_col + c) * n_day + d, (c * n_row + r) * n_day + d)
        for r in range(n_row) for c in range(n_col) for d in range(n_day)
    ]
    turned = lax.ppermute(pair, AXES, turn)
    col_side = lax.all_to_all(jnp.broadcast_to(turned[None], (n_row,) + turned.shape), "row", 0, 0, tiled=True)
    row_side = lax.all_gather(pair, "col", axis=0)
    return stack(place, row_side, col_side)[None, None]


def solution(mesh):
    placed = (P("day", None, ("row", "col"), None), P("day", None, ("row", "col")))
    return jax.shard_map(
        body,
        mesh=mesh,
        in_specs=placed,
        out_specs=P("row", "col", None, "day", None),
        check_vma=False,
    )
```

time: 291 us -> 69.2 us (0.24)
  the two profiles are of different devices: /device:TPU:1 before, /device:TPU:3 now
where the time goes in v1:
time: 69.2 us; the launch traced here: 68.9 us
  blocking collectives  27.4 us (40%)
  starting transfers between devices  25.3 us (37%)
  Pallas kernels  13.7 us (20%)
  local copies, waits for them, and re-layouts  2.4 us (3%)
    all_to_all x1, starting transfers between devices, body(): lax.all_to_all(jnp.broadcast_to(turned[None], (n_row,) + turned.shape), '...  24.6 us
    all_gather x1, blocking collectives, body(): row_side = lax.all_gather(pair, 'col', axis=0)  23.9 us
    pallas_call x1, Pallas kernels, stack(): pl.pallas_call(stack_kernel, grid=(4,), in_specs=[pl.BlockSpec(memory_spa...  12.2 us
    all_gather x1, blocking collectives, body(): pair = lax.all_gather(white, 'day', axis=0)  3.55 us
    pallas_call x1, Pallas kernels, whiten(): pl.pallas_call(whiten_kernel, out_shape=jax.ShapeDtypeStruct((96, 128), j...  1.46 us
  transfers between devices with their start and end apart: 2, of which 0 were waited for; matrix products, arithmetic and copies ran while one was open for 0% of the time, Pallas kernels for 0%

profile of v1, /device:TPU:3, one launch (start us, length us, event | category | flops | bytes accessed | tf_op | source)
XLA Modules:
  0.0 68.9 jit_solution(11580580883914945492)
XLA Ops:
  0.0 1.3 %copy.5.avail_ref = s32[1,6,4]{2,1,0:T(8,128)} copy(s32[1,6,4]{1,2,0:T(4,128)} %param.4) | data formatting | bytes 192 | tf_op args[1]
  1.4 1.5 %whiten.1 = bf16[96,128]{1,0:T(8,128)(2,1)} custom-call(bf16[1,6,4,512]{3,2,1,0:T(4,128)(2,1)} %spec_ref.1, s32[1,6,4]{2,1,0:T(8,128)} %copy.5.avail_ref), custom_call_target="tpu_custom_call" | custom-call | tf_op jit(solution)/shard_map/whiten/pallas_call | solution.py:42
  2.8 3.6 %all-gather = bf16[192,128]{1,0:T(8,128)(2,1)S(1)} all-gather(bf16[96,128]{1,0:T(8,128)(2,1)} %whiten.1), channel_id=2, replica_groups=mesh['row'=16,'col'=16,'day'=2] {'day'}, dimensions={0}, use_global_device_ids=true | all-gather | bytes 73728 | tf_op jit(solution)/shard_map/all_gather | solution.py:196
  6.4 0.7 collective-permute-start
  7.0 0.0 collective-permute-done
  7.0 1.0 %broadcast_in_dim.4 = bf16[16,2,96,128]{3,2,1,0:T(8,128)(2,1)} broadcast(bf16[2,96,128]{2,1,0:T(8,128)(2,1)S(1)} %collective-permute-done), dimensions={1,2,3} | broadcast | bytes 835584 | tf_op jit(solution)/shard_map/broadcast_in_dim | solution.py:202
  8.1 24.6 %all-to-all-start = ((bf16[16,2,96,128]{3,2,1,0:T(8,128)(2,1)}), bf16[16,2,96,128]{3,2,1,0:T(8,128)(2,1)S(1)}, u32[]{:S(2)}, u32[]{:S(2)}) async-start(bf16[16,2,96,128]{3,2,1,0:T(8,128)(2,1)} %broadcast_in_dim.4), calls=%async_computation | async-start | bytes 1572864 | tf_op jit(solution)/shard_map/all_to_all | solution.py:202
  32.7 0.1 pad_add_fusion.place_ref
  32.8 0.0 copy-start
  32.8 23.9 %all-gather.1 = bf16[32,96,128]{2,1,0:T(8,128)(2,1)S(1)} all-gather(bf16[2,96,128]{2,1,0:T(8,128)(2,1)S(1)} %bitcast.8), channel_id=3, replica_groups=mesh['row'=16,'col'=16,'day'=2] {'col'}, dimensions={0}, use_global_device_ids=true | all-gather | bytes 835584 | tf_op jit(solution)/shard_map/all_gather | solution.py:203
  56.7 0.0 all-to-all-done.col_ref
  56.7 0.0 copy-done
  56.7 12.2 %stack.17 = bf16[32,32,128]{2,1,0:T(8,128)(2,1)} custom-call(s32[3]{0:T(128)S(1)} %pad_add_fusion.place_ref, bf16[16,2,96,128]{3,2,1,0:T(8,128)(2,1)S(1)} %bitcast.6, bf16[16,2,96,128]{3,2,1,0:T(8,128)(2,1)S(1)} %all-to-all-done.col_ref, bf16[512,256]{1,0:T(8,128)(2,1)S(1)} %copy-done), custom_call_target="tpu_custom_call" | custom-call | tf_op jit(solution)/shard_map/stack/pallas_call | solution.py:170
Async XLA Ops:
  6.4 0.7 collective-permute-start
  8.1 48.6 %all-to-all-start = ((bf16[16,2,96,128]{3,2,1,0:T(8,128)(2,1)}), bf16[16,2,96,128]{3,2,1,0:T(8,128)(2,1)S(1)}, u32[]{:S(2)}, u32[]{:S(2)}) async-start(bf16[16,2,96,128]{3,2,1,0:T(8,128)(2,1)} %broadcast_in_dim.4), calls=%async_computation | async-start | bytes 1572864 | tf_op jit(solution)/shard_map/all_to_all | solution.py:202
  32.8 23.9 %copy-start = (bf16[512,256]{1,0:T(8,128)(2,1)S(1)}, bf16[512,256]{1,0:T(8,128)(2,1)}, u32[]{:S(2)}) copy-start(bf16[512,256]{1,0:T(8,128)(2,1)} %constant.14.clone.table_ref) | copy-start | bytes 786436

commit v2 on v1

v2 whole, which is shorter than its diff:
```python
import math

import jax
import jax.numpy as jnp
import ml_dtypes
import numpy as np
from jax import lax
from jax.experimental import pallas as pl
from jax.experimental.pallas import tpu as pltpu
from jax.sharding import PartitionSpec as P

BINS = 256
LAGS = 128
HOURS = 6
AXES = ("row", "col", "day")
DT = jnp.bfloat16
G = 16
CH = 32
UN = 4


def lag_table():
    freq = (np.arange(BINS) + 0.5) * (math.pi / BINS)
    angles = freq[:, None] * (np.arange(LAGS) - LAGS // 2)[None, :]
    upper = np.concatenate([np.cos(angles), np.sin(angles)], 1)
    lower = np.concatenate([-np.sin(angles), np.cos(angles)], 1)
    return (np.concatenate([upper, lower], 0) / math.sqrt(HOURS * BINS)).astype(ml_dtypes.bfloat16)

def whiten_kernel(spec_ref, avail_ref, out_ref, rows):
    avail = avail_ref[0].astype(jnp.float32)
    for h in range(HOURS):
        x = spec_ref[0, h].astype(jnp.float32)
        re, im = x[:, :BINS], x[:, BINS:]
        power = re * re + im * im
        level = jnp.mean(power, axis=1, keepdims=True) + 1e-06
        factor = avail[:, h:h + 1] * lax.rsqrt(power + 0.09 * level)
        white = (re * factor, im * factor)
        for part in range(4):
            piece = white[part // 2][:, (part % 2) * 128:(part % 2) * 128 + 128]
            rows[pl.ds(part * 24 + h, 4, stride=6), :] = piece
    out_ref[...] = rows[...].astype(jnp.bfloat16)

def whiten(spectra, avail):
    return pl.pallas_call(
        whiten_kernel,
        out_shape=jax.ShapeDtypeStruct((96, 128), jnp.bfloat16),
        scratch_shapes=[pltpu.VMEM((96, 128), jnp.float32)],
        name="whiten",
    )(spectra, avail.transpose(0, 2, 1))

def tree(terms):
    while len(terms) > 1:
        terms = [terms[i] + terms[i + 1] if i + 1 < len(terms) else terms[i] for i in range(0, len(terms), 2)]
    return terms[0]


def stack_kernel(place_ref, row_ref, col_ref, table_ref, out_ref, rows, firsts, seconds, cross):
    below = place_ref[0] > place_ref[1]
    day_id = place_ref[2]
    corner = jnp.logical_and(place_ref[0] == place_ref[1], day_id == 0)
    ones = jnp.full((LAGS, LAGS), 1.0, jnp.bfloat16)

    def split_hours(source):
        for day in range(2):
            for h in range(HOURS):
                for part in range(4):
                    v = rows[part, pl.ds(day * 192 + h, 32, stride=6), :]
                    if source == 1 and part >= 2:
                        v = -v
                    seconds[source, day, h, part] = v.astype(DT)

    @pl.loop(0, 8, unroll=2)
    def _(j):
        for day in range(2):
            at = pl.ds(pl.multiple_of(day * 192 + j * 24, 8), 24)
            first = jnp.where(below, col_ref[j + 8, day], row_ref[j, day]).astype(jnp.float32)
            second = jnp.where(below, row_ref[j + 8 * day_id, day], col_ref[j + 8 * day_id, day]).astype(jnp.float32)
            for part in range(4):
                firsts[part, at, :] = first[part * 24:part * 24 + 24]
                rows[part, at, :] = second[part * 24:part * 24 + 24]

    split_hours(0)

    @pl.when(corner)
    def _():
        @pl.loop(0, 8, unroll=2)
        def _(j):
            for day in range(2):
                at = pl.ds(pl.multiple_of(day * 192 + j * 24, 8), 24)
                first_at = pl.ds(pl.multiple_of(384 + day * 192 + j * 24, 8), 24)
                other = row_ref[j + 8, day].astype(jnp.float32)
                for part in range(4):
                    piece = other[part * 24:part * 24 + 24]
                    rows[part, at, :] = piece
                    firsts[part, first_at, :] = piece if part < 2 else -piece

        split_hours(1)

    def tile(source, day, a, q):
        at = source * 384 + day * 192 + a * 6
        parts = [None] * 4
        for k in range(2):
            re, im = [], []
            for h in range(HOURS):
                fr, fi = (
                    jnp.broadcast_to(firsts[part, pl.ds(at + h, 1), :], (G, 128)).astype(DT) for part in (k, k + 2)
                )
                sr, si = (seconds[source, day, h, part, q * G:(q + 1) * G, :] for part in (k, k + 2))
                re.append(fr * sr + fi * si)
                im.append(fi * sr - fr * si)
            parts[k], parts[k + 2] = tree(re), tree(im)
        return jnp.concatenate(parts, axis=1).astype(jnp.bfloat16)

    def fill(a, slot):
        for day in range(2):
            for q in range(32 // G):
                source = jnp.where(jnp.logical_and(corner, a // G > q), 1, 0)
                at = pl.ds(pl.multiple_of(slot * 32 + q * G, G), G)
                cross[day, at, :] = tile(source, day, a, q)

    def mend(a, slot):
        j = lax.broadcasted_iota(jnp.int32, (G, 512), 0)
        q = a // G
        inner = a - q * G
        for day in range(2):
            at = pl.ds(pl.multiple_of(slot * 32 + q * G, G), G)
            other = corner_tile(day, a, q).astype(jnp.float32)
            own = cross[day, at, :].astype(jnp.float32)
            own = jnp.where(j < inner, other, jnp.where(j == inner, 0.0, own))
            cross[day, at, :] = own.astype(jnp.bfloat16)

    def corner_tile(day, a, q):
        at = 384 + day * 192 + a * 6
        parts = [None] * 4
        for k in range(2):
            re, im = [], []
            for h in range(HOURS):
                fr, fi = (
                    jnp.broadcast_to(firsts[part, pl.ds(at + h, 1), :], (G, 128)).astype(DT) for part in (k, k + 2)
                )
                sr, si = (seconds[1, day, h, part, pl.ds(pl.multiple_of(q * G, G), G), :] for part in (k, k + 2))
                re.append(fr * sr + fi * si)
                im.append(fi * sr - fr * si)
            parts[k], parts[k + 2] = tree(re), tree(im)
        return jnp.concatenate(parts, axis=1).astype(jnp.bfloat16)

    def finish(a):
        table = table_ref[...]
        lin = re = im = None
        for day in range(2):
            both = jnp.dot(cross[day], table, preferred_element_type=jnp.float32)
            corr, hilb = both[:, :LAGS], both[:, LAGS:]
            amp = corr * corr + hilb * hilb
            spread = jnp.dot(amp.astype(jnp.bfloat16), ones, preferred_element_type=jnp.float32) * (1.0 / LAGS) + 1e-06
            inverse = lax.rsqrt(amp + 0.01 * spread)
            if day == 0:
                lin, re, im = corr, corr * inverse, hilb * inverse
            else:
                lin, re, im = lin + corr, re + corr * inverse, im + hilb * inverse
        stacked = (lin * (re * re + im * im) * 0.25).astype(jnp.bfloat16)
        out_ref[pl.ds(pl.multiple_of(a, CH), CH)] = stacked.reshape(CH, 32, LAGS)

    @pl.loop(0, 32 // CH)
    def _(i):
        @pl.loop(0, CH, unroll=UN)
        def _(slot):
            fill(i * CH + slot, slot)

        @pl.when(corner)
        def _():
            @pl.loop(0, CH, unroll=UN)
            def _(slot):
                mend(i * CH + slot, slot)

        finish(i * CH)


def stack(place, row_side, col_side):
    vmem = pl.BlockSpec(memory_space=pltpu.VMEM)
    return pl.pallas_call(
        stack_kernel,
        in_specs=[pl.BlockSpec(memory_space=pltpu.SMEM), vmem, vmem, vmem],
        out_specs=vmem,
        out_shape=jax.ShapeDtypeStruct((32, 32, LAGS), jnp.bfloat16),
        scratch_shapes=[
            pltpu.VMEM((4, 384, 128), jnp.float32),
            pltpu.VMEM((4, 768, 128), jnp.float32),
            pltpu.VMEM((2, 2, HOURS, 4, 32, 128), DT),
            pltpu.VMEM((2, CH * 32, 512), jnp.bfloat16),
        ],
        compiler_params=pltpu.CompilerParams(vmem_limit_bytes=32 * 1024 * 1024),
        name="stack",
    )(place, row_side, col_side, jnp.asarray(lag_table()))


def body(spectra, avail):
    n_row, n_col, n_day = (lax.axis_size(name) for name in AXES)
    place = jnp.stack([lax.axis_index(name) for name in AXES]).astype(jnp.int32)
    white = whiten(spectra, avail)
    pair = lax.all_gather(white, "day", axis=0)
    turn = [
        ((r * n_col + c) * n_day + d, (c * n_row + r) * n_day + d)
        for r in range(n_row) for c in range(n_col) for d in range(n_day)
    ]
    turned = lax.ppermute(pair, AXES, turn)
    col_side = lax.all_to_all(jnp.broadcast_to(turned[None], (n_row,) + turned.shape), "row", 0, 0, tiled=True)
    row_side = lax.all_gather(pair, "col", axis=0)
    return stack(place, row_side, col_side)[None, None]


def solution(mesh):
    placed = (P("day", None, ("row", "col"), None), P("day", None, ("row", "col")))
    return jax.shard_map(
        body,
        mesh=mesh,
        in_specs=placed,
        out_specs=P("row", "col", None, "day", None),
        check_vma=False,
    )
```

time: 69.2 us -> 62.7 us (0.906)
  Pallas kernels: 13.7 us -> 8.53 us
  local copies, waits for them, and re-layouts: 2.4 us -> 1.05 us
    pallas_call x1, Pallas kernels: 12.2 us -> 7.03 us  [stack(): pl.pallas_call(stack_kernel, in_specs=[pl.BlockSpec(memory_space=pltpu.SM...]
    unnamed x3 -> x2, local copies, waits for them, and re-layouts: 1.35 us -> 0.01 us
where the time goes in v2:
time: 62.7 us; the launch traced here: 62.4 us
  blocking collectives  27.4 us (44%)
  starting transfers between devices  25.3 us (40%)
  Pallas kernels  8.53 us (14%)
  local copies, waits for them, and re-layouts  1.05 us (2%)
    all_to_all x1, starting transfers between devices, body(): lax.all_to_all(jnp.broadcast_to(turned[None], (n_row,) + turned.shape), '...  24.6 us
    all_gather x1, blocking collectives, body(): row_side = lax.all_gather(pair, 'col', axis=0)  23.9 us
    pallas_call x1, Pallas kernels, stack(): pl.pallas_call(stack_kernel, in_specs=[pl.BlockSpec(memory_space=pltpu.SM...  7.03 us
    all_gather x1, blocking collectives, body(): pair = lax.all_gather(white, 'day', axis=0)  3.55 us
    pallas_call x1, Pallas kernels, whiten(): pl.pallas_call(whiten_kernel, out_shape=jax.ShapeDtypeStruct((96, 128), j...  1.49 us
  transfers between devices with their start and end apart: 2, of which 0 were waited for; matrix products, arithmetic and copies ran while one was open for 0% of the time, Pallas kernels for 0%

profile of v2, /device:TPU:3, one launch (start us, length us, event | category | flops | bytes accessed | tf_op | source)
XLA Modules:
  0.0 62.4 jit_solution(8996606637199473285)
XLA Ops:
  0.0 1.5 %whiten.1 = bf16[96,128]{1,0:T(8,128)(2,1)} custom-call(bf16[1,6,4,512]{3,2,1,0:T(4,128)(2,1)} %spec_ref.1, s32[1,4,6]{2,1,0:T(4,128)} %bitcast.10), custom_call_target="tpu_custom_call" | custom-call | tf_op jit(solution)/shard_map/whiten/pallas_call | solution.py:44
  1.5 3.6 %all-gather = bf16[192,128]{1,0:T(8,128)(2,1)S(1)} all-gather(bf16[96,128]{1,0:T(8,128)(2,1)} %whiten.1), channel_id=2, replica_groups=mesh['row'=16,'col'=16,'day'=2] {'day'}, dimensions={0}, use_global_device_ids=true | all-gather | bytes 73728 | tf_op jit(solution)/shard_map/all_gather | solution.py:200
  5.0 0.7 %collective-permute-start = (bf16[2,96,128]{2,1,0:T(8,128)(2,1)S(1)}, bf16[2,96,128]{2,1,0:T(8,128)(2,1)S(1)}, u32[]{:S(2)}, u32[]{:S(2)}) collective-permute-start(bf16[2,96,128]{2,1,0:T(8,128)(2,1)S(1)} %bitcast.8), channel_id=1, source_target_pairs={{0,0},{1,1},{2,32},{3,33},{4,64},{5,65},{6,96},{7,97},{8,128},{9,1... | collective-permute-start | bytes 147464 | tf_op jit(solution)/shard_map/ppermute | solution.py:205
  5.7 0.0 collective-permute-done
  5.7 1.0 %broadcast_in_dim.4 = bf16[16,2,96,128]{3,2,1,0:T(8,128)(2,1)} broadcast(bf16[2,96,128]{2,1,0:T(8,128)(2,1)S(1)} %collective-permute-done), dimensions={1,2,3} | broadcast | bytes 835584 | tf_op jit(solution)/shard_map/broadcast_in_dim | solution.py:206
  6.8 24.6 %all-to-all-start = ((bf16[16,2,96,128]{3,2,1,0:T(8,128)(2,1)}), bf16[16,2,96,128]{3,2,1,0:T(8,128)(2,1)S(1)}, u32[]{:S(2)}, u32[]{:S(2)}) async-start(bf16[16,2,96,128]{3,2,1,0:T(8,128)(2,1)} %broadcast_in_dim.4), calls=%async_computation | async-start | bytes 1572864 | tf_op jit(solution)/shard_map/all_to_all | solution.py:206
  31.4 0.1 pad_add_fusion.place_ref
  31.5 0.0 copy-start
  31.5 23.9 %all-gather.1 = bf16[32,96,128]{2,1,0:T(8,128)(2,1)S(1)} all-gather(bf16[2,96,128]{2,1,0:T(8,128)(2,1)S(1)} %bitcast.9), channel_id=3, replica_groups=mesh['row'=16,'col'=16,'day'=2] {'col'}, dimensions={0}, use_global_device_ids=true | all-gather | bytes 835584 | tf_op jit(solution)/shard_map/all_gather | solution.py:207
  55.3 0.0 all-to-all-done.col_ref
  55.3 0.0 copy-done
  55.4 7.0 %stack.17 = bf16[32,32,128]{2,1,0:T(8,128)(2,1)} custom-call(s32[3]{0:T(128)S(1)} %pad_add_fusion.place_ref, bf16[16,2,96,128]{3,2,1,0:T(8,128)(2,1)S(1)} %bitcast.7, bf16[16,2,96,128]{3,2,1,0:T(8,128)(2,1)S(1)} %all-to-all-done.col_ref, bf16[512,256]{1,0:T(8,128)(2,1)S(1)} %copy-done), custom_call_target="tpu_custom_call" | custom-call | tf_op jit(solution)/shard_map/stack/pallas_call | solution.py:180
Async XLA Ops:
  5.0 0.7 %collective-permute-start = (bf16[2,96,128]{2,1,0:T(8,128)(2,1)S(1)}, bf16[2,96,128]{2,1,0:T(8,128)(2,1)S(1)}, u32[]{:S(2)}, u32[]{:S(2)}) collective-permute-start(bf16[2,96,128]{2,1,0:T(8,128)(2,1)S(1)} %bitcast.8), channel_id=1, source_target_pairs={{0,0},{1,1},{2,32},{3,33},{4,64},{5,65},{6,96},{7,97},{8,128},{9,1... | collective-permute-start | bytes 147464 | tf_op jit(solution)/shard_map/ppermute | solution.py:205
  6.8 48.6 %all-to-all-start = ((bf16[16,2,96,128]{3,2,1,0:T(8,128)(2,1)}), bf16[16,2,96,128]{3,2,1,0:T(8,128)(2,1)S(1)}, u32[]{:S(2)}, u32[]{:S(2)}) async-start(bf16[16,2,96,128]{3,2,1,0:T(8,128)(2,1)} %broadcast_in_dim.4), calls=%async_computation | async-start | bytes 1572864 | tf_op jit(solution)/shard_map/all_to_all | solution.py:206
  31.5 23.9 %copy-start = (bf16[512,256]{1,0:T(8,128)(2,1)S(1)}, bf16[512,256]{1,0:T(8,128)(2,1)}, u32[]{:S(2)}) copy-start(bf16[512,256]{1,0:T(8,128)(2,1)} %constant.14.clone.table_ref) | copy-start | bytes 786436

commit v3 on v2

--- a/solution.py
+++ b/solution.py
@@ -16,7 +16,8 @@
 DT = jnp.bfloat16
 G = 16
 CH = 32
-UN = 4
+UN = 8
+UC = 4
 
 
 def lag_table():
@@ -56,6 +57,7 @@
 
 def stack_kernel(place_ref, row_ref, col_ref, table_ref, out_ref, rows, firsts, seconds, cross):
     below = place_ref[0] > place_ref[1]
+    above = place_ref[0] < place_ref[1]
     day_id = place_ref[2]
     corner = jnp.logical_and(place_ref[0] == place_ref[1], day_id == 0)
     ones = jnp.full((LAGS, LAGS), 1.0, jnp.bfloat16)
@@ -73,8 +75,8 @@
     def _(j):
         for day in range(2):
             at = pl.ds(pl.multiple_of(day * 192 + j * 24, 8), 24)
-            first = jnp.where(below, col_ref[j + 8, day], row_ref[j, day]).astype(jnp.float32)
-            second = jnp.where(below, row_ref[j + 8 * day_id, day], col_ref[j + 8 * day_id, day]).astype(jnp.float32)
+            first = jnp.where(below, col_ref[2 * j + day], row_ref[j, day]).astype(jnp.float32)
+            second = jnp.where(above, col_ref[2 * j + day], row_ref[j + 8 * day_id, day]).astype(jnp.float32)
             for part in range(4):
                 firsts[part, at, :] = first[part * 24:part * 24 + 24]
                 rows[part, at, :] = second[part * 24:part * 24 + 24]
@@ -96,53 +98,42 @@
 
         split_hours(1)
 
-    def tile(source, day, a, q):
-        at = source * 384 + day * 192 + a * 6
-        parts = [None] * 4
-        for k in range(2):
-            re, im = [], []
-            for h in range(HOURS):
-                fr, fi = (
-                    jnp.broadcast_to(firsts[part, pl.ds(at + h, 1), :], (G, 128)).astype(DT) for part in (k, k + 2)
-                )
-                sr, si = (seconds[source, day, h, part, q * G:(q + 1) * G, :] for part in (k, k + 2))
-                re.append(fr * sr + fi * si)
-                im.append(fi * sr - fr * si)
-            parts[k], parts[k + 2] = tree(re), tree(im)
-        return jnp.concatenate(parts, axis=1).astype(jnp.bfloat16)
-
-    def fill(a, slot):
-        for day in range(2):
-            for q in range(32 // G):
-                source = jnp.where(jnp.logical_and(corner, a // G > q), 1, 0)
-                at = pl.ds(pl.multiple_of(slot * 32 + q * G, G), G)
-                cross[day, at, :] = tile(source, day, a, q)
-
-    def mend(a, slot):
-        j = lax.broadcasted_iota(jnp.int32, (G, 512), 0)
-        q = a // G
-        inner = a - q * G
-        for day in range(2):
-            at = pl.ds(pl.multiple_of(slot * 32 + q * G, G), G)
-            other = corner_tile(day, a, q).astype(jnp.float32)
-            own = cross[day, at, :].astype(jnp.float32)
-            own = jnp.where(j < inner, other, jnp.where(j == inner, 0.0, own))
-            cross[day, at, :] = own.astype(jnp.bfloat16)
-
-    def corner_tile(day, a, q):
-        at = 384 + day * 192 + a * 6
-        parts = [None] * 4
-        for k in range(2):
-            re, im = [], []
-            for h in range(HOURS):
-                fr, fi = (
-                    jnp.broadcast_to(firsts[part, pl.ds(at + h, 1), :], (G, 128)).astype(DT) for part in (k, k + 2)
-                )
-                sr, si = (seconds[1, day, h, part, pl.ds(pl.multiple_of(q * G, G), G), :] for part in (k, k + 2))
-                re.append(fr * sr + fi * si)
-                im.append(fi * sr - fr * si)
-            parts[k], parts[k + 2] = tree(re), tree(im)
-        return jnp.concatenate(parts, axis=1).astype(jnp.bfloat16)
+    def fill(a, plan):
+        mark = lax.broadcasted_iota(jnp.int32, (G, 128), 0)
+        inner = lax.rem(a, G)
+        for day in range(2):
+            parts = [[None] * 4 for _ in plan]
+            for k in range(2):
+                re, im = [[] for _ in plan], [[] for _ in plan]
+                for h in range(HOURS):
+                    at = day * 192 + a * 6 + h
+                    wanted = sorted({s for p in plan for s in ((0, 1) if p is None else (p,))})
+                    first = {
+                        s: [
+                            jnp.broadcast_to(firsts[part, pl.ds(s * 384 + at, 1), :], (G, 128)).astype(DT)
+                            for part in (k, k + 2)
+                        ]
+                        for s in wanted
+                    }
+                    for q, p in enumerate(plan):
+                        def second(s, part):
+                            return seconds[s, day, h, part, q * G:(q + 1) * G, :]
+
+                        if p is None:
+                            fr, fi = (jnp.where(mark < inner, y, x) for x, y in zip(first[0], first[1]))
+                            sr, si = (jnp.where(mark < inner, second(1, part), second(0, part)) for part in (k, k + 2))
+                        else:
+                            fr, fi = first[p]
+                            sr, si = (second(p, part) for part in (k, k + 2))
+                        re[q].append(fr * sr + fi * si)
+                        im[q].append(fi * sr - fr * si)
+                for q, p in enumerate(plan):
+                    for part, terms in ((k, re[q]), (k + 2, im[q])):
+                        total = tree(terms)
+                        if p is None:
+                            total = jnp.where(mark == inner, jnp.zeros_like(total), total)
+                        at = pl.ds(pl.multiple_of(a * 32 + q * G, G), G)
+                        cross[day, at, part * 128:part * 128 + 128] = total.astype(jnp.bfloat16)
 
     def finish(a):
         table = table_ref[...]
@@ -160,19 +151,23 @@
         stacked = (lin * (re * re + im * im) * 0.25).astype(jnp.bfloat16)
         out_ref[pl.ds(pl.multiple_of(a, CH), CH)] = stacked.reshape(CH, 32, LAGS)
 
-    @pl.loop(0, 32 // CH)
-    def _(i):
-        @pl.loop(0, CH, unroll=UN)
-        def _(slot):
-            fill(i * CH + slot, slot)
-
-        @pl.when(corner)
-        def _():
-            @pl.loop(0, CH, unroll=UN)
-            def _(slot):
-                mend(i * CH + slot, slot)
-
-        finish(i * CH)
+    @pl.when(corner)
+    def _():
+        @pl.loop(0, G, unroll=UC)
+        def _(a):
+            fill(a, (None, 0))
+
+        @pl.loop(G, 2 * G, unroll=UC)
+        def _(a):
+            fill(a, (1, None))
+
+    @pl.when(jnp.logical_not(corner))
+    def _():
+        @pl.loop(0, 32, unroll=UN)
+        def _(a):
+            fill(a, (0, 0))
+
+    finish(0)
 
 
 def stack(place, row_side, col_side):
@@ -195,17 +190,21 @@
 
 def body(spectra, avail):
     n_row, n_col, n_day = (lax.axis_size(name) for name in AXES)
-    place = jnp.stack([lax.axis_index(name) for name in AXES]).astype(jnp.int32)
+    row_id, col_id, day_id = place = [lax.axis_index(name) for name in AXES]
     white = whiten(spectra, avail)
-    pair = lax.all_gather(white, "day", axis=0)
+    half = n_col // 2
     turn = [
-        ((r * n_col + c) * n_day + d, (c * n_row + r) * n_day + d)
-        for r in range(n_row) for c in range(n_col) for d in range(n_day)
+        ((c * n_col + s) * n_day + day, ((s % half * n_day + day) * n_col + c) * n_day + s // half)
+        for c in range(n_row) for s in range(n_col) for day in range(n_day)
     ]
-    turned = lax.ppermute(pair, AXES, turn)
-    col_side = lax.all_to_all(jnp.broadcast_to(turned[None], (n_row,) + turned.shape), "row", 0, 0, tiled=True)
-    row_side = lax.all_gather(pair, "col", axis=0)
-    return stack(place, row_side, col_side)[None, None]
+    turned = lax.ppermute(white, AXES, turn)
+    days = lax.all_gather(white, "day", axis=0)
+    turned, days = lax.optimization_barrier((turned, days))
+    halves = lax.all_gather(turned, "day", axis=0)
+    upper = jnp.logical_or(lax.broadcasted_iota(jnp.int32, (n_row, 1, 1), 0) > col_id, day_id == 1)
+    col_side = lax.all_to_all(jnp.where(upper, halves[1], halves[0]), "row", 0, 0, tiled=True)
+    row_side = lax.all_gather(days, "col", axis=0)
+    return stack(jnp.stack(place).astype(jnp.int32), row_side, col_side)[None, None]
 
 
 def solution(mesh):

time: 62.7 us -> 61.9 us (0.987)
  starting transfers between devices: 25.3 us -> 13.8 us
  blocking collectives: 27.4 us -> 38.5 us
  local copies, waits for them, and re-layouts: 1.05 us -> 0.01 us
  other arithmetic: 0.08 us -> 0.93 us
    all_to_all x1, starting transfers between devices: 24.6 us -> 10.7 us  [body(): lax.all_to_all(jnp.where(upper, halves[1], halves[0]), 'row', 0, 0, tiled...]
    all_gather x2 -> x3, blocking collectives: 27.4 us -> 38.5 us  [the longest x1 25.2 us: body(): row_side = lax.all_gather(days, 'col', axis=0)]
    ppermute x1, starting transfers between devices: 0.65 us -> 3.11 us  [body(): turned = lax.ppermute(white, AXES, turn)]
    broadcast_in_dim x1 -> x0, local copies, waits for them, and re-layouts: 1.04 us -> none  [body(): jnp.broadcast_to(turned[None], (n_row,) + turned.shape)]
    select_n x0 -> x1, other arithmetic: none -> 0.84 us  [body(): jnp.where(upper, halves[1], halves[0])]
where the time goes in v3:
time: 61.9 us; the launch traced here: 61.5 us
  blocking collectives  38.5 us (62%)
  starting transfers between devices  13.8 us (22%)
  Pallas kernels  8.2 us (13%)
  other arithmetic  0.93 us (2%)
    all_gather x1, blocking collectives, body(): row_side = lax.all_gather(days, 'col', axis=0)  25.2 us
    all_to_all x1, starting transfers between devices, body(): lax.all_to_all(jnp.where(upper, halves[1], halves[0]), 'row', 0, 0, tiled...  10.7 us
    all_gather x1, blocking collectives, body(): halves = lax.all_gather(turned, 'day', axis=0)  9.37 us
    pallas_call x1, Pallas kernels, stack(): pl.pallas_call(stack_kernel, in_specs=[pl.BlockSpec(memory_space=pltpu.SM...  6.7 us
    all_gather x1, blocking collectives, body(): days = lax.all_gather(white, 'day', axis=0)  3.98 us
    ppermute x1, starting transfers between devices, body(): turned = lax.ppermute(white, AXES, turn)  3.11 us
    pallas_call x1, Pallas kernels, whiten(): pl.pallas_call(whiten_kernel, out_shape=jax.ShapeDtypeStruct((96, 128), j...  1.49 us
  transfers between devices with their start and end apart: 2, of which 0 were waited for; matrix products, arithmetic and copies ran while one was open for 0% of the time, Pallas kernels for 0%

profile of v3, /device:TPU:3, one launch (start us, length us, event | category | flops | bytes accessed | tf_op | source)
XLA Modules:
  0.0 61.5 jit_solution(4344025452379446318)
XLA Ops:
  0.0 1.5 %whiten.1 = bf16[96,128]{1,0:T(8,128)(2,1)} custom-call(bf16[1,6,4,512]{3,2,1,0:T(4,128)(2,1)} %spec_ref.1, s32[1,4,6]{2,1,0:T(4,128)} %bitcast.9), custom_call_target="tpu_custom_call" | custom-call | tf_op jit(solution)/shard_map/whiten/pallas_call | solution.py:45
  1.5 3.1 %collective-permute-start = (bf16[96,128]{1,0:T(8,128)(2,1)}, bf16[96,128]{1,0:T(8,128)(2,1)S(1)}, u32[]{:S(2)}, u32[]{:S(2)}) collective-permute-start(bf16[96,128]{1,0:T(8,128)(2,1)} %whiten.1), channel_id=1, source_target_pairs={{0,0},{1,32},{2,64},{3,96},{4,128},{5,160},{6,192},{7,224},{8,256}... | collective-permute-start | bytes 73736 | tf_op jit(solution)/shard_map/ppermute | solution.py:200
  4.6 4.0 %all-gather = bf16[192,128]{1,0:T(8,128)(2,1)S(1)} all-gather(bf16[96,128]{1,0:T(8,128)(2,1)} %whiten.1), channel_id=2, replica_groups=mesh['row'=16,'col'=16,'day'=2] {'day'}, dimensions={0}, use_global_device_ids=true | all-gather | bytes 73728 | tf_op jit(solution)/shard_map/all_gather | solution.py:201
  8.6 0.0 collective-permute-done
  8.6 9.4 %all-gather.2 = bf16[192,128]{1,0:T(8,128)(2,1)S(1)} all-gather(bf16[96,128]{1,0:T(8,128)(2,1)S(1)} %collective-permute-done), channel_id=4, replica_groups=mesh['row'=16,'col'=16,'day'=2] {'day'}, dimensions={0}, use_global_device_ids=true | all-gather | bytes 73728 | tf_op jit(solution)/shard_map/all_gather | solution.py:203
  18.0 0.8 %broadcast_select_fusion = bf16[16,96,128]{2,1,0:T(8,128)(2,1)} fusion(pred[16]{0:T(512)(128)(4,1)S(1)} %compare_or_fusion, bf16[96,128]{1,0:T(8,128)(2,1)S(1)} %get-tuple-element.10, bf16[96,128]{1,0:T(8,128)(2,1)S(1)} %get-tuple-element.9), kind=kLoop, calls=%fused_computation | loop fusion | flops 196608 | bytes 442384 | tf_op jit(solution)/shard_map/jit(_where)/select_n | solution.py:205
  18.8 10.7 %all-to-all-start = ((bf16[16,96,128]{2,1,0:T(8,128)(2,1)}), bf16[16,96,128]{2,1,0:T(8,128)(2,1)S(1)}, u32[]{:S(2)}, u32[]{:S(2)}) async-start(bf16[16,96,128]{2,1,0:T(8,128)(2,1)} %broadcast_select_fusion), calls=%async_computation | async-start | bytes 786432 | tf_op jit(solution)/shard_map/all_to_all | solution.py:205
  29.6 0.1 pad_add_fusion.place_ref
  29.6 0.0 copy-start
  29.7 25.2 %all-gather.1 = bf16[32,96,128]{2,1,0:T(8,128)(2,1)S(1)} all-gather(bf16[2,96,128]{2,1,0:T(8,128)(2,1)S(1)} %bitcast.8), channel_id=3, replica_groups=mesh['row'=16,'col'=16,'day'=2] {'col'}, dimensions={0}, use_global_device_ids=true | all-gather | bytes 835584 | tf_op jit(solution)/shard_map/all_gather | solution.py:206
  54.8 0.0 all-to-all-done.col_ref
  54.8 0.0 copy-done
  54.8 6.7 %stack.17 = bf16[32,32,128]{2,1,0:T(8,128)(2,1)} custom-call(s32[3]{0:T(128)S(1)} %pad_add_fusion.place_ref, bf16[16,2,96,128]{3,2,1,0:T(8,128)(2,1)S(1)} %bitcast.7, bf16[16,96,128]{2,1,0:T(8,128)(2,1)S(1)} %all-to-all-done.col_ref, bf16[512,256]{1,0:T(8,128)(2,1)S(1)} %copy-done), custom_call_target="tpu_custom_call" | custom-call | tf_op jit(solution)/shard_map/stack/pallas_call | solution.py:175
  (2 shorter events, 0.0 us)
Async XLA Ops:
  1.5 7.1 %collective-permute-start = (bf16[96,128]{1,0:T(8,128)(2,1)}, bf16[96,128]{1,0:T(8,128)(2,1)S(1)}, u32[]{:S(2)}, u32[]{:S(2)}) collective-permute-start(bf16[96,128]{1,0:T(8,128)(2,1)} %whiten.1), channel_id=1, source_target_pairs={{0,0},{1,32},{2,64},{3,96},{4,128},{5,160},{6,192},{7,224},{8,256}... | collective-permute-start | bytes 73736 | tf_op jit(solution)/shard_map/ppermute | solution.py:200
  18.8 36.0 %all-to-all-start = ((bf16[16,96,128]{2,1,0:T(8,128)(2,1)}), bf16[16,96,128]{2,1,0:T(8,128)(2,1)S(1)}, u32[]{:S(2)}, u32[]{:S(2)}) async-start(bf16[16,96,128]{2,1,0:T(8,128)(2,1)} %broadcast_select_fusion), calls=%async_computation | async-start | bytes 786432 | tf_op jit(solution)/shard_map/all_to_all | solution.py:205
  29.6 25.2 %copy-start = (bf16[512,256]{1,0:T(8,128)(2,1)S(1)}, bf16[512,256]{1,0:T(8,128)(2,1)}, u32[]{:S(2)}) copy-start(bf16[512,256]{1,0:T(8,128)(2,1)} %constant.16.clone.table_ref) | copy-start | bytes 786436

commit v4 on v3

--- a/solution.py
+++ b/solution.py
@@ -13,6 +13,7 @@
 LAGS = 128
 HOURS = 6
 AXES = ("row", "col", "day")
+MOVE = (11, 10, 14, 9, 13, 15, 3, 2, 0, 1, 4, 12, 6, 8, 5, 7)
 DT = jnp.bfloat16
 G = 16
 CH = 32
@@ -59,8 +60,15 @@
     below = place_ref[0] > place_ref[1]
     above = place_ref[0] < place_ref[1]
     day_id = place_ref[2]
+    col_start = jnp.where(above, 8 * day_id, 8)
     corner = jnp.logical_and(place_ref[0] == place_ref[1], day_id == 0)
     ones = jnp.full((LAGS, LAGS), 1.0, jnp.bfloat16)
+
+    def held(shard):
+        move = shard ^ place_ref[1]
+        words = [sum(m << 4 * i for i, m in enumerate(MOVE[at:at + 8])) for at in (0, 8)]
+        word = jnp.where(move < 8, words[0], words[1])
+        return (lax.shift_right_logical(word, 4 * (move & 7)) & 15) ^ place_ref[1]
 
     def split_hours(source):
         for day in range(2):
@@ -75,8 +83,9 @@
     def _(j):
         for day in range(2):
             at = pl.ds(pl.multiple_of(day * 192 + j * 24, 8), 24)
-            first = jnp.where(below, col_ref[2 * j + day], row_ref[j, day]).astype(jnp.float32)
-            second = jnp.where(above, col_ref[2 * j + day], row_ref[j + 8 * day_id, day]).astype(jnp.float32)
+            from_col = col_ref[held(col_start + j), day]
+            first = jnp.where(below, from_col, row_ref[j, day]).astype(jnp.float32)
+            second = jnp.where(above, from_col, row_ref[j + 8 * day_id, day]).astype(jnp.float32)
             for part in range(4):
                 firsts[part, at, :] = first[part * 24:part * 24 + 24]
                 rows[part, at, :] = second[part * 24:part * 24 + 24]
@@ -190,21 +199,20 @@
 
 def body(spectra, avail):
     n_row, n_col, n_day = (lax.axis_size(name) for name in AXES)
-    row_id, col_id, day_id = place = [lax.axis_index(name) for name in AXES]
+    row_id, col_id, day_id = (lax.axis_index(name) for name in AXES)
     white = whiten(spectra, avail)
-    half = n_col // 2
     turn = [
-        ((c * n_col + s) * n_day + day, ((s % half * n_day + day) * n_col + c) * n_day + s // half)
+        ((c * n_col + s) * n_day + day, ((c ^ MOVE[s ^ c]) * n_col + c) * n_day + day)
         for c in range(n_row) for s in range(n_col) for day in range(n_day)
     ]
     turned = lax.ppermute(white, AXES, turn)
     days = lax.all_gather(white, "day", axis=0)
     turned, days = lax.optimization_barrier((turned, days))
-    halves = lax.all_gather(turned, "day", axis=0)
-    upper = jnp.logical_or(lax.broadcasted_iota(jnp.int32, (n_row, 1, 1), 0) > col_id, day_id == 1)
-    col_side = lax.all_to_all(jnp.where(upper, halves[1], halves[0]), "row", 0, 0, tiled=True)
+    pieces = jnp.broadcast_to(turned[None], (n_row * n_day,) + turned.shape)
+    col_side = lax.all_to_all(pieces, ("row", "day"), 0, 0, tiled=True).reshape((n_row, n_day) + turned.shape)
     row_side = lax.all_gather(days, "col", axis=0)
-    return stack(jnp.stack(place).astype(jnp.int32), row_side, col_side)[None, None]
+    place = jnp.stack([row_id, col_id, day_id]).astype(jnp.int32)
+    return stack(place, row_side, col_side)[None, None]
 
 
 def solution(mesh):

time: 61.9 us -> 57.4 us (0.927)
  the two profiles are of different devices: /device:TPU:3 before, /device:TPU:68 now
where the time goes in v4:
time: 57.4 us; the launch traced here: 57.1 us
  blocking collectives  24.5 us (43%)
  starting transfers between devices  20.6 us (36%)
  Pallas kernels  8.19 us (14%)
  waiting for transfers between devices  2.69 us (5%)
  local copies, waits for them, and re-layouts  1 us (2%)
    all_gather x1, blocking collectives, body(): row_side = lax.all_gather(days, 'col', axis=0)  19.8 us
    all_to_all x1, starting transfers between devices, body(): lax.all_to_all(pieces, ('row', 'day'), 0, 0, tiled=True)  12.9 us
    ppermute x1, starting transfers between devices, body(): turned = lax.ppermute(white, AXES, turn)  7.69 us
    pallas_call x1, Pallas kernels, stack(): pl.pallas_call(stack_kernel, in_specs=[pl.BlockSpec(memory_space=pltpu.SM...  6.7 us
    all_gather x1, blocking collectives, body(): days = lax.all_gather(white, 'day', axis=0)  4.72 us
    all_to_all x1, waiting for transfers between devices, body(): lax.all_to_all(pieces, ('row', 'day'), 0, 0, tiled=True)  2.69 us
    pallas_call x1, Pallas kernels, whiten(): pl.pallas_call(whiten_kernel, out_shape=jax.ShapeDtypeStruct((96, 128), j...  1.49 us
  transfers between devices with their start and end apart: 2, of which 1 were waited for; matrix products, arithmetic and copies ran while one was open for 0% of the time, Pallas kernels for 0%

profile of v4, /device:TPU:68, one launch (start us, length us, event | category | flops | bytes accessed | tf_op | source)
XLA Modules:
  0.0 57.1 jit_solution(10773943406489364491)
XLA Ops:
  0.0 1.5 %whiten.1 = bf16[96,128]{1,0:T(8,128)(2,1)} custom-call(bf16[1,6,4,512]{3,2,1,0:T(4,128)(2,1)} %spec_ref.1, s32[1,4,6]{2,1,0:T(4,128)} %bitcast.11), custom_call_target="tpu_custom_call" | custom-call | tf_op jit(solution)/shard_map/whiten/pallas_call | solution.py:46
  1.5 7.7 %collective-permute-start = (bf16[96,128]{1,0:T(8,128)(2,1)}, bf16[96,128]{1,0:T(8,128)(2,1)S(1)}, u32[]{:S(2)}, u32[]{:S(2)}) collective-permute-start(bf16[96,128]{1,0:T(8,128)(2,1)} %whiten.1), channel_id=1, source_target_pairs={{0,352},{1,353},{2,320},{3,321},{4,448},{5,449},{6,288},{7,289},{8... | collective-permute-start | bytes 73736 | tf_op jit(solution)/shard_map/ppermute | solution.py:208
  9.2 4.7 %all-gather = bf16[192,128]{1,0:T(8,128)(2,1)S(1)} all-gather(bf16[96,128]{1,0:T(8,128)(2,1)} %whiten.1), channel_id=2, replica_groups=mesh['row'=16,'col'=16,'day'=2] {'day'}, dimensions={0}, use_global_device_ids=true | all-gather | bytes 73728 | tf_op jit(solution)/shard_map/all_gather | solution.py:209
  13.9 0.0 collective-permute-done
  13.9 1.0 %broadcast_in_dim.4 = bf16[32,96,128]{2,1,0:T(8,128)(2,1)} broadcast(bf16[96,128]{1,0:T(8,128)(2,1)S(1)} %collective-permute-done), dimensions={1,2} | broadcast | bytes 811008 | tf_op jit(solution)/shard_map/broadcast_in_dim | solution.py:211
  14.9 12.9 %all-to-all-start = ((bf16[32,96,128]{2,1,0:T(8,128)(2,1)}), bf16[32,96,128]{2,1,0:T(8,128)(2,1)S(1)}, u32[]{:S(2)}, u32[]{:S(2)}) async-start(bf16[32,96,128]{2,1,0:T(8,128)(2,1)} %broadcast_in_dim.4), calls=%async_computation | async-start | bytes 1572864 | tf_op jit(solution)/shard_map/all_to_all | solution.py:212
  27.9 0.1 pad_add_fusion.place_ref
  27.9 0.0 copy-start
  27.9 19.8 %all-gather.1 = bf16[32,96,128]{2,1,0:T(8,128)(2,1)S(1)} all-gather(bf16[2,96,128]{2,1,0:T(8,128)(2,1)S(1)} %bitcast.10), channel_id=3, replica_groups=mesh['row'=16,'col'=16,'day'=2] {'col'}, dimensions={0}, use_global_device_ids=true | all-gather | bytes 835584 | tf_op jit(solution)/shard_map/all_gather | solution.py:213
  47.7 2.7 %all-to-all-done = bf16[32,96,128]{2,1,0:T(8,128)(2,1)S(1)} async-done(((bf16[32,96,128]{2,1,0:T(8,128)(2,1)}), bf16[32,96,128]{2,1,0:T(8,128)(2,1)S(1)}, u32[]{:S(2)}, u32[]{:S(2)}) %all-to-all-start) | async-done | bytes 786464 | tf_op jit(solution)/shard_map/all_to_all | solution.py:212
  50.4 0.0 copy-done
  50.4 6.7 %stack.17 = bf16[32,32,128]{2,1,0:T(8,128)(2,1)} custom-call(s32[3]{0:T(128)S(1)} %pad_add_fusion.place_ref, bf16[16,2,96,128]{3,2,1,0:T(8,128)(2,1)S(1)} %bitcast.9, bf16[16,2,96,128]{3,2,1,0:T(8,128)(2,1)S(1)} %bitcast.8, bf16[512,256]{1,0:T(8,128)(2,1)S(1)} %copy-done), custom_call_target="tpu_custom_call" | custom-call | tf_op jit(solution)/shard_map/stack/pallas_call | solution.py:184
Async XLA Ops:
  1.5 12.4 %collective-permute-start = (bf16[96,128]{1,0:T(8,128)(2,1)}, bf16[96,128]{1,0:T(8,128)(2,1)S(1)}, u32[]{:S(2)}, u32[]{:S(2)}) collective-permute-start(bf16[96,128]{1,0:T(8,128)(2,1)} %whiten.1), channel_id=1, source_target_pairs={{0,352},{1,353},{2,320},{3,321},{4,448},{5,449},{6,288},{7,289},{8... | collective-permute-start | bytes 73736 | tf_op jit(solution)/shard_map/ppermute | solution.py:208
  14.9 35.5 %all-to-all-start = ((bf16[32,96,128]{2,1,0:T(8,128)(2,1)}), bf16[32,96,128]{2,1,0:T(8,128)(2,1)S(1)}, u32[]{:S(2)}, u32[]{:S(2)}) async-start(bf16[32,96,128]{2,1,0:T(8,128)(2,1)} %broadcast_in_dim.4), calls=%async_computation | async-start | bytes 1572864 | tf_op jit(solution)/shard_map/all_to_all | solution.py:212
  27.9 22.5 %copy-start = (bf16[512,256]{1,0:T(8,128)(2,1)S(1)}, bf16[512,256]{1,0:T(8,128)(2,1)}, u32[]{:S(2)}) copy-start(bf16[512,256]{1,0:T(8,128)(2,1)} %constant.14.clone.table_ref) | copy-start | bytes 786436

commit v5 on v4

--- a/solution.py
+++ b/solution.py
@@ -18,7 +18,7 @@
 G = 16
 CH = 32
 UN = 8
-UC = 4
+UC = 8
 
 
 def lag_table():
@@ -56,19 +56,18 @@
     return terms[0]
 
 
-def stack_kernel(place_ref, row_ref, col_ref, table_ref, out_ref, rows, firsts, seconds, cross):
-    below = place_ref[0] > place_ref[1]
-    above = place_ref[0] < place_ref[1]
-    day_id = place_ref[2]
+def stack_kernel(row_ref, col_ref, table_ref, out_ref, rows, firsts, seconds, cross):
+    row_id, col_id, day_id = (lax.axis_index(name) for name in AXES)
+    below = row_id > col_id
+    above = row_id < col_id
     col_start = jnp.where(above, 8 * day_id, 8)
-    corner = jnp.logical_and(place_ref[0] == place_ref[1], day_id == 0)
-    ones = jnp.full((LAGS, LAGS), 1.0, jnp.bfloat16)
+    corner = jnp.logical_and(row_id == col_id, day_id == 0)
 
     def held(shard):
-        move = shard ^ place_ref[1]
+        move = shard ^ col_id
         words = [sum(m << 4 * i for i, m in enumerate(MOVE[at:at + 8])) for at in (0, 8)]
         word = jnp.where(move < 8, words[0], words[1])
-        return (lax.shift_right_logical(word, 4 * (move & 7)) & 15) ^ place_ref[1]
+        return (lax.shift_right_logical(word, 4 * (move & 7)) & 15) ^ col_id
 
     def split_hours(source):
         for day in range(2):
@@ -108,8 +107,8 @@
         split_hours(1)
 
     def fill(a, plan):
-        mark = lax.broadcasted_iota(jnp.int32, (G, 128), 0)
-        inner = lax.rem(a, G)
+        mark = lax.broadcasted_iota(jnp.int16, (G, 128), 0)
+        inner = jnp.full((G, 128), lax.rem(a, G), jnp.int32).astype(jnp.int16)
         for day in range(2):
             parts = [[None] * 4 for _ in plan]
             for k in range(2):
@@ -151,8 +150,8 @@
             both = jnp.dot(cross[day], table, preferred_element_type=jnp.float32)
             corr, hilb = both[:, :LAGS], both[:, LAGS:]
             amp = corr * corr + hilb * hilb
-            spread = jnp.dot(amp.astype(jnp.bfloat16), ones, preferred_element_type=jnp.float32) * (1.0 / LAGS) + 1e-06
-            inverse = lax.rsqrt(amp + 0.01 * spread)
+            spread = jnp.sum(amp, axis=1, keepdims=True) * (0.01 / LAGS) + 1e-08
+            inverse = lax.rsqrt(amp + spread)
             if day == 0:
                 lin, re, im = corr, corr * inverse, hilb * inverse
             else:
@@ -179,11 +178,11 @@
     finish(0)
 
 
-def stack(place, row_side, col_side):
+def stack(row_side, col_side):
     vmem = pl.BlockSpec(memory_space=pltpu.VMEM)
     return pl.pallas_call(
         stack_kernel,
-        in_specs=[pl.BlockSpec(memory_space=pltpu.SMEM), vmem, vmem, vmem],
+        in_specs=[vmem, vmem, vmem],
         out_specs=vmem,
         out_shape=jax.ShapeDtypeStruct((32, 32, LAGS), jnp.bfloat16),
         scratch_shapes=[
@@ -194,12 +193,11 @@
         ],
         compiler_params=pltpu.CompilerParams(vmem_limit_bytes=32 * 1024 * 1024),
         name="stack",
-    )(place, row_side, col_side, jnp.asarray(lag_table()))
+    )(row_side, col_side, jnp.asarray(lag_table()))
 
 
 def body(spectra, avail):
     n_row, n_col, n_day = (lax.axis_size(name) for name in AXES)
-    row_id, col_id, day_id = (lax.axis_index(name) for name in AXES)
     white = whiten(spectra, avail)
     turn = [
         ((c * n_col + s) * n_day + day, ((c ^ MOVE[s ^ c]) * n_col + c) * n_day + day)
@@ -211,8 +209,7 @@
     pieces = jnp.broadcast_to(turned[None], (n_row * n_day,) + turned.shape)
     col_side = lax.all_to_all(pieces, ("row", "day"), 0, 0, tiled=True).reshape((n_row, n_day) + turned.shape)
     row_side = lax.all_gather(days, "col", axis=0)
-    place = jnp.stack([row_id, col_id, day_id]).astype(jnp.int32)
-    return stack(place, row_side, col_side)[None, None]
+    return stack(row_side, col_side)[None, None]
 
 
 def solution(mesh):

time: 57.4 us -> 55.6 us (0.969)
  Pallas kernels: 8.19 us -> 6.39 us
    pallas_call x1, Pallas kernels: 6.7 us -> 4.89 us  [stack(): pl.pallas_call(stack_kernel, in_specs=[vmem, vmem, vmem], out_specs=vmem,...]
where the time goes in v5:
time: 55.6 us; the launch traced here: 55.3 us
  blocking collectives  24.5 us (44%)
  starting transfers between devices  20.6 us (37%)
  Pallas kernels  6.39 us (11%)
  waiting for transfers between devices  2.74 us (5%)
  local copies, waits for them, and re-layouts  1 us (2%)
    all_gather x1, blocking collectives, body(): row_side = lax.all_gather(days, 'col', axis=0)  19.8 us
    all_to_all x1, starting transfers between devices, body(): lax.all_to_all(pieces, ('row', 'day'), 0, 0, tiled=True)  12.9 us
    ppermute x1, starting transfers between devices, body(): turned = lax.ppermute(white, AXES, turn)  7.69 us
    pallas_call x1, Pallas kernels, stack(): pl.pallas_call(stack_kernel, in_specs=[vmem, vmem, vmem], out_specs=vmem,...  4.89 us
    all_gather x1, blocking collectives, body(): days = lax.all_gather(white, 'day', axis=0)  4.72 us
    all_to_all x1, waiting for transfers between devices, body(): lax.all_to_all(pieces, ('row', 'day'), 0, 0, tiled=True)  2.74 us
    pallas_call x1, Pallas kernels, whiten(): pl.pallas_call(whiten_kernel, out_shape=jax.ShapeDtypeStruct((96, 128), j...  1.49 us
  transfers between devices with their start and end apart: 2, of which 1 were waited for; matrix products, arithmetic and copies ran while one was open for 0% of the time, Pallas kernels for 0%

profile of v5, /device:TPU:68, one launch (start us, length us, event | category | flops | bytes accessed | tf_op | source)
XLA Modules:
  0.0 55.3 jit_solution(6590472504457879956)
XLA Ops:
  0.0 1.5 %whiten.1 = bf16[96,128]{1,0:T(8,128)(2,1)} custom-call(bf16[1,6,4,512]{3,2,1,0:T(4,128)(2,1)} %spec_ref.1, s32[1,4,6]{2,1,0:T(4,128)} %bitcast.8), custom_call_target="tpu_custom_call" | custom-call | tf_op jit(solution)/shard_map/whiten/pallas_call | solution.py:46
  1.5 7.7 %collective-permute-start = (bf16[96,128]{1,0:T(8,128)(2,1)}, bf16[96,128]{1,0:T(8,128)(2,1)S(1)}, u32[]{:S(2)}, u32[]{:S(2)}) collective-permute-start(bf16[96,128]{1,0:T(8,128)(2,1)} %whiten.1), channel_id=1, source_target_pairs={{0,352},{1,353},{2,320},{3,321},{4,448},{5,449},{6,288},{7,289},{8... | collective-permute-start | bytes 73736 | tf_op jit(solution)/shard_map/ppermute | solution.py:206
  9.2 4.7 %all-gather = bf16[192,128]{1,0:T(8,128)(2,1)S(1)} all-gather(bf16[96,128]{1,0:T(8,128)(2,1)} %whiten.1), channel_id=2, replica_groups=mesh['row'=16,'col'=16,'day'=2] {'day'}, dimensions={0}, use_global_device_ids=true | all-gather | bytes 73728 | tf_op jit(solution)/shard_map/all_gather | solution.py:207
  13.9 0.0 collective-permute-done
  13.9 1.0 %broadcast_in_dim.4 = bf16[32,96,128]{2,1,0:T(8,128)(2,1)} broadcast(bf16[96,128]{1,0:T(8,128)(2,1)S(1)} %collective-permute-done), dimensions={1,2} | broadcast | bytes 811008 | tf_op jit(solution)/shard_map/broadcast_in_dim | solution.py:209
  14.9 12.9 %all-to-all-start = ((bf16[32,96,128]{2,1,0:T(8,128)(2,1)}), bf16[32,96,128]{2,1,0:T(8,128)(2,1)S(1)}, u32[]{:S(2)}, u32[]{:S(2)}) async-start(bf16[32,96,128]{2,1,0:T(8,128)(2,1)} %broadcast_in_dim.4), calls=%async_computation | async-start | bytes 1572864 | tf_op jit(solution)/shard_map/all_to_all | solution.py:210
  27.9 0.0 copy-start
  27.9 19.8 %all-gather.1 = bf16[32,96,128]{2,1,0:T(8,128)(2,1)S(1)} all-gather(bf16[2,96,128]{2,1,0:T(8,128)(2,1)S(1)} %bitcast.7), channel_id=3, replica_groups=mesh['row'=16,'col'=16,'day'=2] {'col'}, dimensions={0}, use_global_device_ids=true | all-gather | bytes 835584 | tf_op jit(solution)/shard_map/all_gather | solution.py:211
  47.7 2.7 %all-to-all-done = bf16[32,96,128]{2,1,0:T(8,128)(2,1)S(1)} async-done(((bf16[32,96,128]{2,1,0:T(8,128)(2,1)}), bf16[32,96,128]{2,1,0:T(8,128)(2,1)S(1)}, u32[]{:S(2)}, u32[]{:S(2)}) %all-to-all-start) | async-done | bytes 786464 | tf_op jit(solution)/shard_map/all_to_all | solution.py:210
  50.4 0.0 copy-done
  50.4 4.9 %stack.1 = bf16[32,32,128]{2,1,0:T(8,128)(2,1)} custom-call(bf16[16,2,96,128]{3,2,1,0:T(8,128)(2,1)S(1)} %bitcast.6, bf16[16,2,96,128]{3,2,1,0:T(8,128)(2,1)S(1)} %bitcast.5, bf16[512,256]{1,0:T(8,128)(2,1)S(1)} %copy-done), custom_call_target="tpu_custom_call" | custom-call | tf_op jit(solution)/shard_map/stack/pallas_call | solution.py:183
Async XLA Ops:
  1.5 12.4 %collective-permute-start = (bf16[96,128]{1,0:T(8,128)(2,1)}, bf16[96,128]{1,0:T(8,128)(2,1)S(1)}, u32[]{:S(2)}, u32[]{:S(2)}) collective-permute-start(bf16[96,128]{1,0:T(8,128)(2,1)} %whiten.1), channel_id=1, source_target_pairs={{0,352},{1,353},{2,320},{3,321},{4,448},{5,449},{6,288},{7,289},{8... | collective-permute-start | bytes 73736 | tf_op jit(solution)/shard_map/ppermute | solution.py:206
  14.9 35.5 %all-to-all-start = ((bf16[32,96,128]{2,1,0:T(8,128)(2,1)}), bf16[32,96,128]{2,1,0:T(8,128)(2,1)S(1)}, u32[]{:S(2)}, u32[]{:S(2)}) async-start(bf16[32,96,128]{2,1,0:T(8,128)(2,1)} %broadcast_in_dim.4), calls=%async_computation | async-start | bytes 1572864 | tf_op jit(solution)/shard_map/all_to_all | solution.py:210
  27.9 22.6 %copy-start = (bf16[512,256]{1,0:T(8,128)(2,1)S(1)}, bf16[512,256]{1,0:T(8,128)(2,1)}, u32[]{:S(2)}) copy-start(bf16[512,256]{1,0:T(8,128)(2,1)} %constant.2.clone.table_ref) | copy-start | bytes 786436

commit v6 on v5

--- a/solution.py
+++ b/solution.py
@@ -13,7 +13,24 @@
 LAGS = 128
 HOURS = 6
 AXES = ("row", "col", "day")
-MOVE = (11, 10, 14, 9, 13, 15, 3, 2, 0, 1, 4, 12, 6, 8, 5, 7)
+HOLDER = (
+    (11, 5, 6, 8, 10, 9, 13, 14, 7, 15, 0, 12, 3, 4, 1, 2),
+    (4, 6, 9, 8, 11, 10, 7, 15, 14, 12, 1, 2, 5, 13, 0, 3),
+    (7, 4, 10, 11, 8, 5, 9, 12, 13, 15, 2, 14, 3, 6, 1, 0),
+    (12, 5, 8, 9, 6, 4, 11, 10, 14, 13, 3, 15, 1, 7, 2, 0),
+    (1, 3, 2, 12, 14, 13, 15, 9, 11, 10, 0, 8, 7, 6, 4, 5),
+    (2, 0, 8, 3, 12, 15, 14, 10, 11, 13, 9, 1, 6, 7, 5, 4),
+    (2, 5, 1, 4, 3, 0, 13, 14, 15, 12, 11, 8, 10, 9, 6, 7),
+    (3, 4, 5, 0, 1, 2, 13, 14, 8, 12, 15, 9, 11, 10, 7, 6),
+    (8, 4, 0, 1, 2, 3, 7, 5, 14, 12, 15, 6, 9, 13, 11, 10),
+    (1, 5, 2, 0, 4, 3, 6, 7, 15, 12, 13, 14, 8, 11, 9, 10),
+    (3, 1, 5, 2, 4, 0, 6, 7, 8, 12, 14, 13, 11, 15, 10, 9),
+    (1, 0, 4, 3, 5, 2, 8, 6, 7, 12, 14, 13, 9, 15, 11, 10),
+    (15, 5, 3, 2, 0, 1, 12, 8, 13, 4, 6, 7, 10, 11, 9, 14),
+    (4, 7, 3, 2, 1, 0, 5, 6, 8, 12, 9, 13, 10, 11, 15, 14),
+    (6, 7, 4, 5, 0, 1, 3, 2, 8, 12, 15, 13, 9, 14, 11, 10),
+    (5, 6, 4, 7, 2, 0, 1, 3, 12, 8, 15, 14, 13, 9, 10, 11),
+)
 DT = jnp.bfloat16
 G = 16
 CH = 32
@@ -64,10 +81,11 @@
     corner = jnp.logical_and(row_id == col_id, day_id == 0)
 
     def held(shard):
-        move = shard ^ col_id
-        words = [sum(m << 4 * i for i, m in enumerate(MOVE[at:at + 8])) for at in (0, 8)]
-        word = jnp.where(move < 8, words[0], words[1])
-        return (lax.shift_right_logical(word, 4 * (move & 7)) & 15) ^ col_id
+        word = jnp.int32(0)
+        for column in range(16):
+            words = [np.uint32(sum(k << 4 * i for i, k in enumerate(HOLDER[column][at:at + 8]))).astype(np.int32) for at in (0, 8)]
+            word = jnp.where(col_id == column, jnp.where(shard < 8, words[0], words[1]), word)
+        return lax.shift_right_logical(word, 4 * (shard & 7)) & 15
 
     def split_hours(source):
         for day in range(2):
@@ -80,9 +98,10 @@
 
     @pl.loop(0, 8, unroll=2)
     def _(j):
+        holder = held(col_start + j)
         for day in range(2):
             at = pl.ds(pl.multiple_of(day * 192 + j * 24, 8), 24)
-            from_col = col_ref[held(col_start + j), day]
+            from_col = col_ref[holder, day]
             first = jnp.where(below, from_col, row_ref[j, day]).astype(jnp.float32)
             second = jnp.where(above, from_col, row_ref[j + 8 * day_id, day]).astype(jnp.float32)
             for part in range(4):
@@ -200,7 +219,7 @@
     n_row, n_col, n_day = (lax.axis_size(name) for name in AXES)
     white = whiten(spectra, avail)
     turn = [
-        ((c * n_col + s) * n_day + day, ((c ^ MOVE[s ^ c]) * n_col + c) * n_day + day)
+        ((c * n_col + s) * n_day + day, (HOLDER[c][s] * n_col + c) * n_day + day)
         for c in range(n_row) for s in range(n_col) for day in range(n_day)
     ]
     turned = lax.ppermute(white, AXES, turn)

time: 55.6 us -> 55.1 us (level)
  the two profiles are of different devices: /device:TPU:68 before, /device:TPU:4 now
where the time goes in v6:
time: 55.1 us; the launch traced here: 54.8 us
  blocking collectives  24.8 us (45%)
  starting transfers between devices  20.8 us (38%)
  Pallas kernels  5.51 us (10%)
  waiting for transfers between devices  2.71 us (5%)
  local copies, waits for them, and re-layouts  1 us (2%)
    all_gather x1, blocking collectives, body(): row_side = lax.all_gather(days, 'col', axis=0)  20.1 us
    all_to_all x1, starting transfers between devices, body(): lax.all_to_all(pieces, ('row', 'day'), 0, 0, tiled=True)  13.9 us
    ppermute x1, starting transfers between devices, body(): turned = lax.ppermute(white, AXES, turn)  6.93 us
    all_gather x1, blocking collectives, body(): days = lax.all_gather(white, 'day', axis=0)  4.72 us
    pallas_call x1, Pallas kernels, stack(): pl.pallas_call(stack_kernel, in_specs=[vmem, vmem, vmem], out_specs=vmem,...  4.02 us
    all_to_all x1, waiting for transfers between devices, body(): lax.all_to_all(pieces, ('row', 'day'), 0, 0, tiled=True)  2.09 us
    pallas_call x1, Pallas kernels, whiten(): pl.pallas_call(whiten_kernel, out_shape=jax.ShapeDtypeStruct((96, 128), j...  1.49 us
  transfers between devices with their start and end apart: 2, of which 2 were waited for; matrix products, arithmetic and copies ran while one was open for 0% of the time, Pallas kernels for 0%

profile of v6, /device:TPU:4, one launch (start us, length us, event | category | flops | bytes accessed | tf_op | source)
XLA Modules:
  0.0 54.8 jit_solution(10582774733472801462)
XLA Ops:
  0.0 1.5 %whiten.1 = bf16[96,128]{1,0:T(8,128)(2,1)} custom-call(bf16[1,6,4,512]{3,2,1,0:T(4,128)(2,1)} %spec_ref.1, s32[1,4,6]{2,1,0:T(4,128)} %bitcast.8), custom_call_target="tpu_custom_call" | custom-call | tf_op jit(solution)/shard_map/whiten/pallas_call | solution.py:63
  1.5 6.9 %collective-permute-start = (bf16[96,128]{1,0:T(8,128)(2,1)}, bf16[96,128]{1,0:T(8,128)(2,1)S(1)}, u32[]{:S(2)}, u32[]{:S(2)}) collective-permute-start(bf16[96,128]{1,0:T(8,128)(2,1)} %whiten.1), channel_id=1, source_target_pairs={{0,352},{1,353},{2,160},{3,161},{4,192},{5,193},{6,256},{7,257},{8... | collective-permute-start | bytes 73736 | tf_op jit(solution)/shard_map/ppermute | solution.py:225
  8.4 4.7 %all-gather = bf16[192,128]{1,0:T(8,128)(2,1)S(1)} all-gather(bf16[96,128]{1,0:T(8,128)(2,1)} %whiten.1), channel_id=2, replica_groups=mesh['row'=16,'col'=16,'day'=2] {'day'}, dimensions={0}, use_global_device_ids=true | all-gather | bytes 73728 | tf_op jit(solution)/shard_map/all_gather | solution.py:226
  13.1 0.6 %collective-permute-done = bf16[96,128]{1,0:T(8,128)(2,1)S(1)} collective-permute-done((bf16[96,128]{1,0:T(8,128)(2,1)}, bf16[96,128]{1,0:T(8,128)(2,1)S(1)}, u32[]{:S(2)}, u32[]{:S(2)}) %collective-permute-start) | collective-permute-done | bytes 24608 | tf_op jit(solution)/shard_map/ppermute | solution.py:225
  13.8 1.0 %broadcast_in_dim.4 = bf16[32,96,128]{2,1,0:T(8,128)(2,1)} broadcast(bf16[96,128]{1,0:T(8,128)(2,1)S(1)} %collective-permute-done), dimensions={1,2} | broadcast | bytes 811008 | tf_op jit(solution)/shard_map/broadcast_in_dim | solution.py:228
  14.8 13.9 %all-to-all-start = ((bf16[32,96,128]{2,1,0:T(8,128)(2,1)}), bf16[32,96,128]{2,1,0:T(8,128)(2,1)S(1)}, u32[]{:S(2)}, u32[]{:S(2)}) async-start(bf16[32,96,128]{2,1,0:T(8,128)(2,1)} %broadcast_in_dim.4), calls=%async_computation | async-start | bytes 1572864 | tf_op jit(solution)/shard_map/all_to_all | solution.py:229
  28.7 0.0 copy-start
  28.7 20.1 %all-gather.1 = bf16[32,96,128]{2,1,0:T(8,128)(2,1)S(1)} all-gather(bf16[2,96,128]{2,1,0:T(8,128)(2,1)S(1)} %bitcast.7), channel_id=3, replica_groups=mesh['row'=16,'col'=16,'day'=2] {'col'}, dimensions={0}, use_global_device_ids=true | all-gather | bytes 835584 | tf_op jit(solution)/shard_map/all_gather | solution.py:230
  48.7 2.1 %all-to-all-done = bf16[32,96,128]{2,1,0:T(8,128)(2,1)S(1)} async-done(((bf16[32,96,128]{2,1,0:T(8,128)(2,1)}), bf16[32,96,128]{2,1,0:T(8,128)(2,1)S(1)}, u32[]{:S(2)}, u32[]{:S(2)}) %all-to-all-start) | async-done | bytes 786464 | tf_op jit(solution)/shard_map/all_to_all | solution.py:229
  50.8 0.0 copy-done
  50.8 4.0 %stack.1 = bf16[32,32,128]{2,1,0:T(8,128)(2,1)} custom-call(bf16[16,2,96,128]{3,2,1,0:T(8,128)(2,1)S(1)} %bitcast.6, bf16[16,2,96,128]{3,2,1,0:T(8,128)(2,1)S(1)} %bitcast.5, bf16[512,256]{1,0:T(8,128)(2,1)S(1)} %copy-done), custom_call_target="tpu_custom_call" | custom-call | tf_op jit(solution)/shard_map/stack/pallas_call | solution.py:202
Async XLA Ops:
  1.5 12.3 %collective-permute-start = (bf16[96,128]{1,0:T(8,128)(2,1)}, bf16[96,128]{1,0:T(8,128)(2,1)S(1)}, u32[]{:S(2)}, u32[]{:S(2)}) collective-permute-start(bf16[96,128]{1,0:T(8,128)(2,1)} %whiten.1), channel_id=1, source_target_pairs={{0,352},{1,353},{2,160},{3,161},{4,192},{5,193},{6,256},{7,257},{8... | collective-permute-start | bytes 73736 | tf_op jit(solution)/shard_map/ppermute | solution.py:225
  14.8 36.1 %all-to-all-start = ((bf16[32,96,128]{2,1,0:T(8,128)(2,1)}), bf16[32,96,128]{2,1,0:T(8,128)(2,1)S(1)}, u32[]{:S(2)}, u32[]{:S(2)}) async-start(bf16[32,96,128]{2,1,0:T(8,128)(2,1)} %broadcast_in_dim.4), calls=%async_computation | async-start | bytes 1572864 | tf_op jit(solution)/shard_map/all_to_all | solution.py:229
  28.7 22.2 %copy-start = (bf16[512,256]{1,0:T(8,128)(2,1)S(1)}, bf16[512,256]{1,0:T(8,128)(2,1)}, u32[]{:S(2)}) copy-start(bf16[512,256]{1,0:T(8,128)(2,1)} %constant.2.clone.table_ref) | copy-start | bytes 786436

commit v7 on v6

--- a/solution.py
+++ b/solution.py
@@ -14,22 +14,22 @@
 HOURS = 6
 AXES = ("row", "col", "day")
 HOLDER = (
-    (11, 5, 6, 8, 10, 9, 13, 14, 7, 15, 0, 12, 3, 4, 1, 2),
-    (4, 6, 9, 8, 11, 10, 7, 15, 14, 12, 1, 2, 5, 13, 0, 3),
-    (7, 4, 10, 11, 8, 5, 9, 12, 13, 15, 2, 14, 3, 6, 1, 0),
-    (12, 5, 8, 9, 6, 4, 11, 10, 14, 13, 3, 15, 1, 7, 2, 0),
-    (1, 3, 2, 12, 14, 13, 15, 9, 11, 10, 0, 8, 7, 6, 4, 5),
-    (2, 0, 8, 3, 12, 15, 14, 10, 11, 13, 9, 1, 6, 7, 5, 4),
-    (2, 5, 1, 4, 3, 0, 13, 14, 15, 12, 11, 8, 10, 9, 6, 7),
-    (3, 4, 5, 0, 1, 2, 13, 14, 8, 12, 15, 9, 11, 10, 7, 6),
-    (8, 4, 0, 1, 2, 3, 7, 5, 14, 12, 15, 6, 9, 13, 11, 10),
-    (1, 5, 2, 0, 4, 3, 6, 7, 15, 12, 13, 14, 8, 11, 9, 10),
-    (3, 1, 5, 2, 4, 0, 6, 7, 8, 12, 14, 13, 11, 15, 10, 9),
-    (1, 0, 4, 3, 5, 2, 8, 6, 7, 12, 14, 13, 9, 15, 11, 10),
-    (15, 5, 3, 2, 0, 1, 12, 8, 13, 4, 6, 7, 10, 11, 9, 14),
-    (4, 7, 3, 2, 1, 0, 5, 6, 8, 12, 9, 13, 10, 11, 15, 14),
-    (6, 7, 4, 5, 0, 1, 3, 2, 8, 12, 15, 13, 9, 14, 11, 10),
-    (5, 6, 4, 7, 2, 0, 1, 3, 12, 8, 15, 14, 13, 9, 10, 11),
+    (11, 10, 14, 9, 5, 2, 6, 8, 0, 3, 1, 15, 13, 7, 4, 12),
+    (11, 10, 15, 8, 6, 4, 9, 7, 1, 2, 0, 3, 12, 14, 5, 13),
+    (0, 9, 11, 8, 10, 12, 7, 4, 5, 3, 2, 1, 13, 6, 14, 15),
+    (13, 0, 10, 9, 8, 11, 6, 4, 7, 1, 3, 2, 12, 5, 14, 15),
+    (4, 0, 1, 3, 15, 14, 13, 10, 12, 11, 8, 2, 7, 5, 9, 6),
+    (0, 1, 2, 3, 15, 14, 13, 11, 10, 12, 8, 7, 5, 6, 4, 9),
+    (2, 5, 1, 3, 11, 15, 12, 13, 14, 8, 9, 0, 10, 4, 7, 6),
+    (4, 3, 2, 0, 12, 15, 13, 14, 9, 10, 11, 8, 1, 5, 7, 6),
+    (4, 8, 11, 9, 10, 1, 13, 6, 14, 2, 3, 15, 7, 0, 12, 5),
+    (8, 5, 6, 4, 12, 1, 2, 0, 15, 3, 14, 7, 11, 13, 10, 9),
+    (8, 6, 10, 9, 5, 7, 4, 2, 3, 1, 13, 12, 15, 0, 14, 11),
+    (7, 10, 11, 8, 4, 6, 0, 3, 5, 2, 13, 1, 14, 12, 15, 9),
+    (14, 2, 13, 3, 12, 15, 1, 0, 4, 8, 5, 9, 10, 6, 11, 7),
+    (3, 9, 1, 0, 13, 12, 14, 2, 15, 8, 5, 4, 11, 7, 6, 10),
+    (8, 5, 0, 9, 3, 1, 14, 13, 2, 15, 10, 12, 6, 7, 11, 4),
+    (7, 10, 14, 13, 3, 0, 15, 12, 2, 1, 11, 8, 4, 9, 6, 5),
 )
 DT = jnp.bfloat16
 G = 16

time: 55.1 us -> 54.6 us (level)
  blocking collectives: 24.8 us -> 23.8 us
  starting transfers between devices: 20.8 us -> 21.4 us
    all_to_all x1, starting transfers between devices: 13.9 us -> 17.2 us  [body(): lax.all_to_all(pieces, ('row', 'day'), 0, 0, tiled=True)]
    ppermute x1, starting transfers between devices: 6.93 us -> 4.21 us  [body(): turned = lax.ppermute(white, AXES, turn)]
    all_gather x1, blocking collectives: 20.1 us -> 19.1 us  [body(): row_side = lax.all_gather(days, 'col', axis=0)]
    ppermute x1, waiting for transfers between devices: 0.62 us -> 0.01 us  [body(): turned = lax.ppermute(white, AXES, turn)]
  transfers between devices with their start and end apart: 2 -> 2, of which waited for: 2 -> 1; matrix products, arithmetic and copies ran while one was open for 0% -> 0% of each run, Pallas kernels for 0% -> 0%
where the time goes in v7:
time: 54.6 us; the launch traced here: 54.3 us
  blocking collectives  23.8 us (44%)
  starting transfers between devices  21.4 us (39%)
  Pallas kernels  5.51 us (10%)
  waiting for transfers between devices  2.58 us (5%)
  local copies, waits for them, and re-layouts  1 us (2%)
    all_gather x1, blocking collectives, body(): row_side = lax.all_gather(days, 'col', axis=0)  19.1 us
    all_to_all x1, starting transfers between devices, body(): lax.all_to_all(pieces, ('row', 'day'), 0, 0, tiled=True)  17.2 us
    all_gather x1, blocking collectives, body(): days = lax.all_gather(white, 'day', axis=0)  4.72 us
    ppermute x1, starting transfers between devices, body(): turned = lax.ppermute(white, AXES, turn)  4.21 us
    pallas_call x1, Pallas kernels, stack(): pl.pallas_call(stack_kernel, in_specs=[vmem, vmem, vmem], out_specs=vmem,...  4.01 us
    all_to_all x1, waiting for transfers between devices, body(): lax.all_to_all(pieces, ('row', 'day'), 0, 0, tiled=True)  2.58 us
    pallas_call x1, Pallas kernels, whiten(): pl.pallas_call(whiten_kernel, out_shape=jax.ShapeDtypeStruct((96, 128), j...  1.49 us
  transfers between devices with their start and end apart: 2, of which 1 were waited for; matrix products, arithmetic and copies ran while one was open for 0% of the time, Pallas kernels for 0%

profile of v7, /device:TPU:4, one launch (start us, length us, event | category | flops | bytes accessed | tf_op | source)
XLA Modules:
  0.0 54.3 jit_solution(10953814949877239123)
XLA Ops:
  0.0 1.5 %whiten.1 = bf16[96,128]{1,0:T(8,128)(2,1)} custom-call(bf16[1,6,4,512]{3,2,1,0:T(4,128)(2,1)} %spec_ref.1, s32[1,4,6]{2,1,0:T(4,128)} %bitcast.8), custom_call_target="tpu_custom_call" | custom-call | tf_op jit(solution)/shard_map/whiten/pallas_call | solution.py:63
  1.5 4.2 %collective-permute-start = (bf16[96,128]{1,0:T(8,128)(2,1)}, bf16[96,128]{1,0:T(8,128)(2,1)S(1)}, u32[]{:S(2)}, u32[]{:S(2)}) collective-permute-start(bf16[96,128]{1,0:T(8,128)(2,1)} %whiten.1), channel_id=1, source_target_pairs={{0,352},{1,353},{2,320},{3,321},{4,448},{5,449},{6,288},{7,289},{8... | collective-permute-start | bytes 73736 | tf_op jit(solution)/shard_map/ppermute | solution.py:225
  5.7 4.7 %all-gather = bf16[192,128]{1,0:T(8,128)(2,1)S(1)} all-gather(bf16[96,128]{1,0:T(8,128)(2,1)} %whiten.1), channel_id=2, replica_groups=mesh['row'=16,'col'=16,'day'=2] {'day'}, dimensions={0}, use_global_device_ids=true | all-gather | bytes 73728 | tf_op jit(solution)/shard_map/all_gather | solution.py:226
  10.4 0.0 collective-permute-done
  10.4 1.0 %broadcast_in_dim.4 = bf16[32,96,128]{2,1,0:T(8,128)(2,1)} broadcast(bf16[96,128]{1,0:T(8,128)(2,1)S(1)} %collective-permute-done), dimensions={1,2} | broadcast | bytes 811008 | tf_op jit(solution)/shard_map/broadcast_in_dim | solution.py:228
  11.4 17.2 %all-to-all-start = ((bf16[32,96,128]{2,1,0:T(8,128)(2,1)}), bf16[32,96,128]{2,1,0:T(8,128)(2,1)S(1)}, u32[]{:S(2)}, u32[]{:S(2)}) async-start(bf16[32,96,128]{2,1,0:T(8,128)(2,1)} %broadcast_in_dim.4), calls=%async_computation | async-start | bytes 1572864 | tf_op jit(solution)/shard_map/all_to_all | solution.py:229
  28.6 0.0 copy-start
  28.6 19.1 %all-gather.1 = bf16[32,96,128]{2,1,0:T(8,128)(2,1)S(1)} all-gather(bf16[2,96,128]{2,1,0:T(8,128)(2,1)S(1)} %bitcast.7), channel_id=3, replica_groups=mesh['row'=16,'col'=16,'day'=2] {'col'}, dimensions={0}, use_global_device_ids=true | all-gather | bytes 835584 | tf_op jit(solution)/shard_map/all_gather | solution.py:230
  47.7 2.6 %all-to-all-done = bf16[32,96,128]{2,1,0:T(8,128)(2,1)S(1)} async-done(((bf16[32,96,128]{2,1,0:T(8,128)(2,1)}), bf16[32,96,128]{2,1,0:T(8,128)(2,1)S(1)}, u32[]{:S(2)}, u32[]{:S(2)}) %all-to-all-start) | async-done | bytes 786464 | tf_op jit(solution)/shard_map/all_to_all | solution.py:229
  50.3 0.0 copy-done
  50.3 4.0 %stack.1 = bf16[32,32,128]{2,1,0:T(8,128)(2,1)} custom-call(bf16[16,2,96,128]{3,2,1,0:T(8,128)(2,1)S(1)} %bitcast.6, bf16[16,2,96,128]{3,2,1,0:T(8,128)(2,1)S(1)} %bitcast.5, bf16[512,256]{1,0:T(8,128)(2,1)S(1)} %copy-done), custom_call_target="tpu_custom_call" | custom-call | tf_op jit(solution)/shard_map/stack/pallas_call | solution.py:202
Async XLA Ops:
  1.5 8.9 %collective-permute-start = (bf16[96,128]{1,0:T(8,128)(2,1)}, bf16[96,128]{1,0:T(8,128)(2,1)S(1)}, u32[]{:S(2)}, u32[]{:S(2)}) collective-permute-start(bf16[96,128]{1,0:T(8,128)(2,1)} %whiten.1), channel_id=1, source_target_pairs={{0,352},{1,353},{2,320},{3,321},{4,448},{5,449},{6,288},{7,289},{8... | collective-permute-start | bytes 73736 | tf_op jit(solution)/shard_map/ppermute | solution.py:225
  11.4 38.8 %all-to-all-start = ((bf16[32,96,128]{2,1,0:T(8,128)(2,1)}), bf16[32,96,128]{2,1,0:T(8,128)(2,1)S(1)}, u32[]{:S(2)}, u32[]{:S(2)}) async-start(bf16[32,96,128]{2,1,0:T(8,128)(2,1)} %broadcast_in_dim.4), calls=%async_computation | async-start | bytes 1572864 | tf_op jit(solution)/shard_map/all_to_all | solution.py:229
  28.6 21.6 %copy-start = (bf16[512,256]{1,0:T(8,128)(2,1)S(1)}, bf16[512,256]{1,0:T(8,128)(2,1)}, u32[]{:S(2)}) copy-start(bf16[512,256]{1,0:T(8,128)(2,1)} %constant.2.clone.table_ref) | copy-start | bytes 786436

commit v8 on v7

--- a/solution.py
+++ b/solution.py
@@ -14,22 +14,22 @@
 HOURS = 6
 AXES = ("row", "col", "day")
 HOLDER = (
-    (11, 10, 14, 9, 5, 2, 6, 8, 0, 3, 1, 15, 13, 7, 4, 12),
-    (11, 10, 15, 8, 6, 4, 9, 7, 1, 2, 0, 3, 12, 14, 5, 13),
-    (0, 9, 11, 8, 10, 12, 7, 4, 5, 3, 2, 1, 13, 6, 14, 15),
-    (13, 0, 10, 9, 8, 11, 6, 4, 7, 1, 3, 2, 12, 5, 14, 15),
-    (4, 0, 1, 3, 15, 14, 13, 10, 12, 11, 8, 2, 7, 5, 9, 6),
-    (0, 1, 2, 3, 15, 14, 13, 11, 10, 12, 8, 7, 5, 6, 4, 9),
-    (2, 5, 1, 3, 11, 15, 12, 13, 14, 8, 9, 0, 10, 4, 7, 6),
-    (4, 3, 2, 0, 12, 15, 13, 14, 9, 10, 11, 8, 1, 5, 7, 6),
-    (4, 8, 11, 9, 10, 1, 13, 6, 14, 2, 3, 15, 7, 0, 12, 5),
-    (8, 5, 6, 4, 12, 1, 2, 0, 15, 3, 14, 7, 11, 13, 10, 9),
-    (8, 6, 10, 9, 5, 7, 4, 2, 3, 1, 13, 12, 15, 0, 14, 11),
-    (7, 10, 11, 8, 4, 6, 0, 3, 5, 2, 13, 1, 14, 12, 15, 9),
-    (14, 2, 13, 3, 12, 15, 1, 0, 4, 8, 5, 9, 10, 6, 11, 7),
-    (3, 9, 1, 0, 13, 12, 14, 2, 15, 8, 5, 4, 11, 7, 6, 10),
-    (8, 5, 0, 9, 3, 1, 14, 13, 2, 15, 10, 12, 6, 7, 11, 4),
-    (7, 10, 14, 13, 3, 0, 15, 12, 2, 1, 11, 8, 4, 9, 6, 5),
+    (11, 10, 9, 14, 6, 8, 7, 5, 4, 13, 0, 12, 2, 15, 1, 3),
+    (10, 11, 9, 8, 6, 7, 4, 15, 0, 12, 1, 13, 5, 14, 2, 3),
+    (10, 4, 11, 9, 12, 8, 15, 7, 6, 5, 2, 0, 13, 1, 3, 14),
+    (8, 5, 10, 9, 13, 11, 14, 6, 7, 4, 3, 0, 15, 12, 2, 1),
+    (12, 2, 15, 13, 10, 14, 9, 11, 6, 8, 1, 3, 4, 0, 7, 5),
+    (8, 3, 12, 11, 15, 14, 10, 13, 9, 2, 0, 7, 4, 1, 5, 6),
+    (1, 2, 0, 3, 9, 11, 15, 13, 12, 14, 8, 10, 7, 4, 6, 5),
+    (3, 0, 2, 1, 12, 9, 14, 13, 10, 15, 11, 8, 6, 5, 7, 4),
+    (4, 8, 12, 0, 3, 1, 2, 13, 14, 6, 10, 15, 11, 7, 9, 5),
+    (5, 1, 4, 0, 2, 3, 12, 7, 14, 15, 11, 6, 10, 13, 9, 8),
+    (6, 7, 5, 2, 1, 3, 4, 0, 15, 12, 8, 13, 11, 14, 10, 9),
+    (0, 4, 3, 8, 12, 7, 2, 1, 6, 5, 15, 13, 9, 14, 11, 10),
+    (4, 2, 3, 1, 0, 12, 15, 13, 8, 14, 5, 7, 10, 6, 9, 11),
+    (5, 4, 12, 2, 1, 0, 13, 3, 8, 14, 6, 9, 11, 7, 10, 15),
+    (4, 7, 5, 15, 0, 14, 2, 1, 3, 12, 13, 8, 9, 6, 10, 11),
+    (6, 5, 7, 4, 2, 0, 3, 12, 15, 1, 14, 13, 8, 11, 10, 9),
 )
 DT = jnp.bfloat16
 G = 16
@@ -64,6 +64,7 @@
         whiten_kernel,
         out_shape=jax.ShapeDtypeStruct((96, 128), jnp.bfloat16),
         scratch_shapes=[pltpu.VMEM((96, 128), jnp.float32)],
+        compiler_params=pltpu.CompilerParams(vmem_limit_bytes=1048576),
         name="whiten",
     )(spectra, avail.transpose(0, 2, 1))
 

time: 54.6 us -> 55.1 us (level)
  local copies, waits for them, and re-layouts: 1 us -> 2.42 us
  Pallas kernels: 5.51 us -> 4.17 us
  blocking collectives: 23.8 us -> 24.5 us
    all_to_all x1, starting transfers between devices: 17.2 us -> 11.6 us  [body(): lax.all_to_all(pieces, ('row', 'day'), 0, 0, tiled=True)]
    ppermute x1, starting transfers between devices: 4.21 us -> 9.54 us  [body(): turned = lax.ppermute(white, AXES, turn)]
    unnamed x2 -> x6, local copies, waits for them, and re-layouts: 0.01 us -> 1.42 us
    pallas_call x1, Pallas kernels: 1.49 us -> 0.15 us  [whiten(): pl.pallas_call(whiten_kernel, out_shape=jax.ShapeDtypeStruct((96, 128), j...]
    all_gather x1, blocking collectives: 19.1 us -> 20 us  [body(): row_side = lax.all_gather(days, 'col', axis=0)]
where the time goes in v8:
time: 55.1 us; the launch traced here: 54.8 us
  blocking collectives  24.5 us (44%)
  starting transfers between devices  21.1 us (38%)
  Pallas kernels  4.17 us (8%)
  waiting for transfers between devices  2.6 us (5%)
  local copies, waits for them, and re-layouts  2.42 us (4%)
    all_gather x1, blocking collectives, body(): row_side = lax.all_gather(days, 'col', axis=0)  20 us
    all_to_all x1, starting transfers between devices, body(): lax.all_to_all(pieces, ('row', 'day'), 0, 0, tiled=True)  11.6 us
    ppermute x1, starting transfers between devices, body(): turned = lax.ppermute(white, AXES, turn)  9.54 us
    all_gather x1, blocking collectives, body(): days = lax.all_gather(white, 'day', axis=0)  4.5 us
    pallas_call x1, Pallas kernels, stack(): pl.pallas_call(stack_kernel, in_specs=[vmem, vmem, vmem], out_specs=vmem,...  4.02 us
    all_to_all x1, waiting for transfers between devices, body(): lax.all_to_all(pieces, ('row', 'day'), 0, 0, tiled=True)  2.59 us
    unnamed x6, local copies, waits for them, and re-layouts  1.42 us
  transfers between devices with their start and end apart: 2, of which 1 were waited for; matrix products, arithmetic and copies ran while one was open for 0% of the time, Pallas kernels for 0%

profile of v8, /device:TPU:4, one launch (start us, length us, event | category | flops | bytes accessed | tf_op | source)
XLA Modules:
  0.0 54.8 jit_solution(1478795645489582208)
XLA Ops:
  0.0 0.0 copy-start.1
  0.0 0.7 %copy-done.1 = bf16[1,6,4,512]{3,2,1,0:T(4,128)(2,1)S(1)} copy-done((bf16[1,6,4,512]{3,2,1,0:T(4,128)(2,1)S(1)}, bf16[1,6,4,512]{3,2,1,0:T(4,128)(2,1)}, u32[]{:S(2)}) %copy-start.1) | copy-done | bytes 24600
  0.7 0.0 copy-start.2
  0.7 0.7 %copy-done.2 = s32[1,6,4]{1,2,0:T(4,128)S(1)} copy-done((s32[1,6,4]{1,2,0:T(4,128)S(1)}, s32[1,6,4]{1,2,0:T(4,128)}, u32[]{:S(2)}) %copy-start.2) | copy-done | bytes 120
  1.4 0.1 whiten.1
  1.6 9.5 %collective-permute-start = (bf16[96,128]{1,0:T(8,128)(2,1)S(1)}, bf16[96,128]{1,0:T(8,128)(2,1)S(1)}, u32[]{:S(2)}, u32[]{:S(2)}) collective-permute-start(bf16[96,128]{1,0:T(8,128)(2,1)S(1)} %whiten.1), channel_id=1, source_target_pairs={{0,352},{1,353},{2,320},{3,321},{4,288},{5,289},{6,448},{7,449},{8... | collective-permute-start | bytes 73736 | tf_op jit(solution)/shard_map/ppermute | solution.py:226
  11.1 4.5 %all-gather = bf16[192,128]{1,0:T(8,128)(2,1)S(1)} all-gather(bf16[96,128]{1,0:T(8,128)(2,1)S(1)} %whiten.1), channel_id=2, replica_groups=mesh['row'=16,'col'=16,'day'=2] {'day'}, dimensions={0}, use_global_device_ids=true | all-gather | bytes 73728 | tf_op jit(solution)/shard_map/all_gather | solution.py:227
  15.6 0.0 collective-permute-done
  15.6 1.0 %broadcast_in_dim.4 = bf16[32,96,128]{2,1,0:T(8,128)(2,1)} broadcast(bf16[96,128]{1,0:T(8,128)(2,1)S(1)} %collective-permute-done), dimensions={1,2} | broadcast | bytes 811008 | tf_op jit(solution)/shard_map/broadcast_in_dim | solution.py:229
  16.6 11.6 %all-to-all-start = ((bf16[32,96,128]{2,1,0:T(8,128)(2,1)}), bf16[32,96,128]{2,1,0:T(8,128)(2,1)S(1)}, u32[]{:S(2)}, u32[]{:S(2)}) async-start(bf16[32,96,128]{2,1,0:T(8,128)(2,1)} %broadcast_in_dim.4), calls=%async_computation | async-start | bytes 1572864 | tf_op jit(solution)/shard_map/all_to_all | solution.py:230
  28.2 0.0 copy-start
  28.2 20.0 %all-gather.1 = bf16[32,96,128]{2,1,0:T(8,128)(2,1)S(1)} all-gather(bf16[2,96,128]{2,1,0:T(8,128)(2,1)S(1)} %bitcast.8), channel_id=3, replica_groups=mesh['row'=16,'col'=16,'day'=2] {'col'}, dimensions={0}, use_global_device_ids=true | all-gather | bytes 835584 | tf_op jit(solution)/shard_map/all_gather | solution.py:231
  48.2 2.6 %all-to-all-done = bf16[32,96,128]{2,1,0:T(8,128)(2,1)S(1)} async-done(((bf16[32,96,128]{2,1,0:T(8,128)(2,1)}), bf16[32,96,128]{2,1,0:T(8,128)(2,1)S(1)}, u32[]{:S(2)}, u32[]{:S(2)}) %all-to-all-start) | async-done | bytes 786464 | tf_op jit(solution)/shard_map/all_to_all | solution.py:230
  50.8 0.0 copy-done
  50.8 4.0 %stack.1 = bf16[32,32,128]{2,1,0:T(8,128)(2,1)} custom-call(bf16[16,2,96,128]{3,2,1,0:T(8,128)(2,1)S(1)} %bitcast.6, bf16[16,2,96,128]{3,2,1,0:T(8,128)(2,1)S(1)} %bitcast.5, bf16[512,256]{1,0:T(8,128)(2,1)S(1)} %copy-done), custom_call_target="tpu_custom_call" | custom-call | tf_op jit(solution)/shard_map/stack/pallas_call | solution.py:203
Async XLA Ops:
  0.0 0.7 %copy-start.1 = (bf16[1,6,4,512]{3,2,1,0:T(4,128)(2,1)S(1)}, bf16[1,6,4,512]{3,2,1,0:T(4,128)(2,1)}, u32[]{:S(2)}) copy-start(bf16[1,6,4,512]{3,2,1,0:T(4,128)(2,1)} %spec_ref.1) | copy-start | bytes 73732
  0.7 0.7 %copy-start.2 = (s32[1,6,4]{1,2,0:T(4,128)S(1)}, s32[1,6,4]{1,2,0:T(4,128)}, u32[]{:S(2)}) copy-start(s32[1,6,4]{1,2,0:T(4,128)} %param.4) | copy-start | bytes 292
  1.6 14.1 %collective-permute-start = (bf16[96,128]{1,0:T(8,128)(2,1)S(1)}, bf16[96,128]{1,0:T(8,128)(2,1)S(1)}, u32[]{:S(2)}, u32[]{:S(2)}) collective-permute-start(bf16[96,128]{1,0:T(8,128)(2,1)S(1)} %whiten.1), channel_id=1, source_target_pairs={{0,352},{1,353},{2,320},{3,321},{4,288},{5,289},{6,448},{7,449},{8... | collective-permute-start | bytes 73736 | tf_op jit(solution)/shard_map/ppermute | solution.py:226
  16.6 34.1 %all-to-all-start = ((bf16[32,96,128]{2,1,0:T(8,128)(2,1)}), bf16[32,96,128]{2,1,0:T(8,128)(2,1)S(1)}, u32[]{:S(2)}, u32[]{:S(2)}) async-start(bf16[32,96,128]{2,1,0:T(8,128)(2,1)} %broadcast_in_dim.4), calls=%async_computation | async-start | bytes 1572864 | tf_op jit(solution)/shard_map/all_to_all | solution.py:230
  28.2 22.6 %copy-start = (bf16[512,256]{1,0:T(8,128)(2,1)S(1)}, bf16[512,256]{1,0:T(8,128)(2,1)}, u32[]{:S(2)}) copy-start(bf16[512,256]{1,0:T(8,128)(2,1)} %constant.2.clone.table_ref) | copy-start | bytes 786436

commit v9 on v8

--- a/solution.py
+++ b/solution.py
@@ -14,22 +14,22 @@
 HOURS = 6
 AXES = ("row", "col", "day")
 HOLDER = (
-    (11, 10, 9, 14, 6, 8, 7, 5, 4, 13, 0, 12, 2, 15, 1, 3),
-    (10, 11, 9, 8, 6, 7, 4, 15, 0, 12, 1, 13, 5, 14, 2, 3),
-    (10, 4, 11, 9, 12, 8, 15, 7, 6, 5, 2, 0, 13, 1, 3, 14),
-    (8, 5, 10, 9, 13, 11, 14, 6, 7, 4, 3, 0, 15, 12, 2, 1),
-    (12, 2, 15, 13, 10, 14, 9, 11, 6, 8, 1, 3, 4, 0, 7, 5),
-    (8, 3, 12, 11, 15, 14, 10, 13, 9, 2, 0, 7, 4, 1, 5, 6),
-    (1, 2, 0, 3, 9, 11, 15, 13, 12, 14, 8, 10, 7, 4, 6, 5),
-    (3, 0, 2, 1, 12, 9, 14, 13, 10, 15, 11, 8, 6, 5, 7, 4),
-    (4, 8, 12, 0, 3, 1, 2, 13, 14, 6, 10, 15, 11, 7, 9, 5),
-    (5, 1, 4, 0, 2, 3, 12, 7, 14, 15, 11, 6, 10, 13, 9, 8),
-    (6, 7, 5, 2, 1, 3, 4, 0, 15, 12, 8, 13, 11, 14, 10, 9),
-    (0, 4, 3, 8, 12, 7, 2, 1, 6, 5, 15, 13, 9, 14, 11, 10),
-    (4, 2, 3, 1, 0, 12, 15, 13, 8, 14, 5, 7, 10, 6, 9, 11),
-    (5, 4, 12, 2, 1, 0, 13, 3, 8, 14, 6, 9, 11, 7, 10, 15),
-    (4, 7, 5, 15, 0, 14, 2, 1, 3, 12, 13, 8, 9, 6, 10, 11),
-    (6, 5, 7, 4, 2, 0, 3, 12, 15, 1, 14, 13, 8, 11, 10, 9),
+    (10, 11, 14, 9, 6, 8, 13, 7, 3, 1, 0, 2, 5, 4, 12, 15),
+    (10, 11, 8, 9, 7, 6, 4, 15, 1, 0, 12, 13, 3, 14, 2, 5),
+    (10, 6, 11, 9, 8, 5, 15, 7, 4, 1, 3, 0, 13, 2, 14, 12),
+    (11, 13, 10, 9, 8, 5, 6, 7, 4, 1, 3, 0, 12, 2, 14, 15),
+    (12, 8, 13, 11, 10, 14, 9, 15, 2, 6, 3, 0, 1, 7, 5, 4),
+    (2, 3, 10, 13, 15, 14, 11, 12, 7, 8, 0, 9, 1, 6, 4, 5),
+    (3, 7, 0, 8, 15, 11, 13, 12, 10, 14, 1, 9, 2, 6, 4, 5),
+    (2, 6, 0, 11, 9, 10, 13, 15, 14, 12, 8, 1, 5, 4, 7, 3),
+    (8, 4, 5, 7, 3, 1, 13, 10, 6, 14, 2, 15, 11, 9, 0, 12),
+    (5, 8, 0, 12, 2, 7, 6, 3, 15, 14, 11, 13, 10, 1, 9, 4),
+    (6, 8, 10, 2, 1, 4, 3, 5, 7, 0, 14, 13, 12, 9, 11, 15),
+    (7, 12, 11, 8, 3, 4, 0, 2, 13, 6, 15, 1, 14, 5, 10, 9),
+    (14, 8, 3, 13, 12, 0, 2, 1, 4, 15, 5, 7, 6, 10, 9, 11),
+    (8, 9, 2, 1, 0, 12, 3, 13, 4, 5, 10, 6, 7, 11, 15, 14),
+    (4, 6, 14, 15, 13, 1, 2, 3, 12, 0, 5, 8, 7, 9, 11, 10),
+    (13, 6, 8, 7, 2, 3, 12, 15, 14, 0, 1, 4, 5, 11, 9, 10),
 )
 DT = jnp.bfloat16
 G = 16

time: 55.1 us -> 54.1 us (0.982)
  blocking collectives: 24.5 us -> 23.9 us
where the time goes in v9:
time: 54.1 us; the launch traced here: 53.8 us
  blocking collectives  23.9 us (44%)
  starting transfers between devices  21.2 us (39%)
  Pallas kernels  4.17 us (8%)
  local copies, waits for them, and re-layouts  2.42 us (4%)
  waiting for transfers between devices  2.05 us (4%)
    all_gather x1, blocking collectives, body(): row_side = lax.all_gather(days, 'col', axis=0)  19.4 us
    all_to_all x1, starting transfers between devices, body(): lax.all_to_all(pieces, ('row', 'day'), 0, 0, tiled=True)  11.6 us
    ppermute x1, starting transfers between devices, body(): turned = lax.ppermute(white, AXES, turn)  9.54 us
    all_gather x1, blocking collectives, body(): days = lax.all_gather(white, 'day', axis=0)  4.5 us
    pallas_call x1, Pallas kernels, stack(): pl.pallas_call(stack_kernel, in_specs=[vmem, vmem, vmem], out_specs=vmem,...  4.02 us
    all_to_all x1, waiting for transfers between devices, body(): lax.all_to_all(pieces, ('row', 'day'), 0, 0, tiled=True)  2.05 us
    unnamed x6, local copies, waits for them, and re-layouts  1.42 us
  transfers between devices with their start and end apart: 2, of which 1 were waited for; matrix products, arithmetic and copies ran while one was open for 0% of the time, Pallas kernels for 0%

profile of v9, /device:TPU:4, one launch (start us, length us, event | category | flops | bytes accessed | tf_op | source)
XLA Modules:
  0.0 53.8 jit_solution(5742069888328683631)
XLA Ops:
  0.0 0.0 copy-start.1
  0.0 0.7 %copy-done.1 = bf16[1,6,4,512]{3,2,1,0:T(4,128)(2,1)S(1)} copy-done((bf16[1,6,4,512]{3,2,1,0:T(4,128)(2,1)S(1)}, bf16[1,6,4,512]{3,2,1,0:T(4,128)(2,1)}, u32[]{:S(2)}) %copy-start.1) | copy-done | bytes 24600
  0.7 0.0 copy-start.2
  0.7 0.7 %copy-done.2 = s32[1,6,4]{1,2,0:T(4,128)S(1)} copy-done((s32[1,6,4]{1,2,0:T(4,128)S(1)}, s32[1,6,4]{1,2,0:T(4,128)}, u32[]{:S(2)}) %copy-start.2) | copy-done | bytes 120
  1.4 0.1 whiten.1
  1.6 9.5 %collective-permute-start = (bf16[96,128]{1,0:T(8,128)(2,1)S(1)}, bf16[96,128]{1,0:T(8,128)(2,1)S(1)}, u32[]{:S(2)}, u32[]{:S(2)}) collective-permute-start(bf16[96,128]{1,0:T(8,128)(2,1)S(1)} %whiten.1), channel_id=1, source_target_pairs={{0,320},{1,321},{2,352},{3,353},{4,448},{5,449},{6,288},{7,289},{8... | collective-permute-start | bytes 73736 | tf_op jit(solution)/shard_map/ppermute | solution.py:226
  11.1 4.5 %all-gather = bf16[192,128]{1,0:T(8,128)(2,1)S(1)} all-gather(bf16[96,128]{1,0:T(8,128)(2,1)S(1)} %whiten.1), channel_id=2, replica_groups=mesh['row'=16,'col'=16,'day'=2] {'day'}, dimensions={0}, use_global_device_ids=true | all-gather | bytes 73728 | tf_op jit(solution)/shard_map/all_gather | solution.py:227
  15.6 0.0 collective-permute-done
  15.6 1.0 %broadcast_in_dim.4 = bf16[32,96,128]{2,1,0:T(8,128)(2,1)} broadcast(bf16[96,128]{1,0:T(8,128)(2,1)S(1)} %collective-permute-done), dimensions={1,2} | broadcast | bytes 811008 | tf_op jit(solution)/shard_map/broadcast_in_dim | solution.py:229
  16.6 11.6 %all-to-all-start = ((bf16[32,96,128]{2,1,0:T(8,128)(2,1)}), bf16[32,96,128]{2,1,0:T(8,128)(2,1)S(1)}, u32[]{:S(2)}, u32[]{:S(2)}) async-start(bf16[32,96,128]{2,1,0:T(8,128)(2,1)} %broadcast_in_dim.4), calls=%async_computation | async-start | bytes 1572864 | tf_op jit(solution)/shard_map/all_to_all | solution.py:230
  28.3 0.0 copy-start
  28.3 19.4 %all-gather.1 = bf16[32,96,128]{2,1,0:T(8,128)(2,1)S(1)} all-gather(bf16[2,96,128]{2,1,0:T(8,128)(2,1)S(1)} %bitcast.8), channel_id=3, replica_groups=mesh['row'=16,'col'=16,'day'=2] {'col'}, dimensions={0}, use_global_device_ids=true | all-gather | bytes 835584 | tf_op jit(solution)/shard_map/all_gather | solution.py:231
  47.7 2.1 %all-to-all-done = bf16[32,96,128]{2,1,0:T(8,128)(2,1)S(1)} async-done(((bf16[32,96,128]{2,1,0:T(8,128)(2,1)}), bf16[32,96,128]{2,1,0:T(8,128)(2,1)S(1)}, u32[]{:S(2)}, u32[]{:S(2)}) %all-to-all-start) | async-done | bytes 786464 | tf_op jit(solution)/shard_map/all_to_all | solution.py:230
  49.8 0.0 copy-done
  49.8 4.0 %stack.1 = bf16[32,32,128]{2,1,0:T(8,128)(2,1)} custom-call(bf16[16,2,96,128]{3,2,1,0:T(8,128)(2,1)S(1)} %bitcast.6, bf16[16,2,96,128]{3,2,1,0:T(8,128)(2,1)S(1)} %bitcast.5, bf16[512,256]{1,0:T(8,128)(2,1)S(1)} %copy-done), custom_call_target="tpu_custom_call" | custom-call | tf_op jit(solution)/shard_map/stack/pallas_call | solution.py:203
Async XLA Ops:
  0.0 0.7 %copy-start.1 = (bf16[1,6,4,512]{3,2,1,0:T(4,128)(2,1)S(1)}, bf16[1,6,4,512]{3,2,1,0:T(4,128)(2,1)}, u32[]{:S(2)}) copy-start(bf16[1,6,4,512]{3,2,1,0:T(4,128)(2,1)} %spec_ref.1) | copy-start | bytes 73732
  0.7 0.7 %copy-start.2 = (s32[1,6,4]{1,2,0:T(4,128)S(1)}, s32[1,6,4]{1,2,0:T(4,128)}, u32[]{:S(2)}) copy-start(s32[1,6,4]{1,2,0:T(4,128)} %param.4) | copy-start | bytes 292
  1.6 14.1 %collective-permute-start = (bf16[96,128]{1,0:T(8,128)(2,1)S(1)}, bf16[96,128]{1,0:T(8,128)(2,1)S(1)}, u32[]{:S(2)}, u32[]{:S(2)}) collective-permute-start(bf16[96,128]{1,0:T(8,128)(2,1)S(1)} %whiten.1), channel_id=1, source_target_pairs={{0,320},{1,321},{2,352},{3,353},{4,448},{5,449},{6,288},{7,289},{8... | collective-permute-start | bytes 73736 | tf_op jit(solution)/shard_map/ppermute | solution.py:226
  16.6 33.1 %all-to-all-start = ((bf16[32,96,128]{2,1,0:T(8,128)(2,1)}), bf16[32,96,128]{2,1,0:T(8,128)(2,1)S(1)}, u32[]{:S(2)}, u32[]{:S(2)}) async-start(bf16[32,96,128]{2,1,0:T(8,128)(2,1)} %broadcast_in_dim.4), calls=%async_computation | async-start | bytes 1572864 | tf_op jit(solution)/shard_map/all_to_all | solution.py:230
  28.3 21.5 %copy-start = (bf16[512,256]{1,0:T(8,128)(2,1)S(1)}, bf16[512,256]{1,0:T(8,128)(2,1)}, u32[]{:S(2)}) copy-start(bf16[512,256]{1,0:T(8,128)(2,1)} %constant.2.clone.table_ref) | copy-start | bytes 786436

commit v10 on v9

--- a/solution.py
+++ b/solution.py
@@ -57,13 +57,13 @@
         for part in range(4):
             piece = white[part // 2][:, (part % 2) * 128:(part % 2) * 128 + 128]
             rows[pl.ds(part * 24 + h, 4, stride=6), :] = piece
-    out_ref[...] = rows[...].astype(jnp.bfloat16)
+    out_ref[...] = rows[:96].astype(jnp.bfloat16)
 
 def whiten(spectra, avail):
     return pl.pallas_call(
         whiten_kernel,
         out_shape=jax.ShapeDtypeStruct((96, 128), jnp.bfloat16),
-        scratch_shapes=[pltpu.VMEM((96, 128), jnp.float32)],
+        scratch_shapes=[pltpu.VMEM((128, 128), jnp.float32)],
         compiler_params=pltpu.CompilerParams(vmem_limit_bytes=1048576),
         name="whiten",
     )(spectra, avail.transpose(0, 2, 1))
@@ -206,8 +206,8 @@
         out_specs=vmem,
         out_shape=jax.ShapeDtypeStruct((32, 32, LAGS), jnp.bfloat16),
         scratch_shapes=[
-            pltpu.VMEM((4, 384, 128), jnp.float32),
-            pltpu.VMEM((4, 768, 128), jnp.float32),
+            pltpu.VMEM((4, 392, 128), jnp.float32),
+            pltpu.VMEM((4, 776, 128), jnp.float32),
             pltpu.VMEM((2, 2, HOURS, 4, 32, 128), DT),
             pltpu.VMEM((2, CH * 32, 512), jnp.bfloat16),
         ],

time: 54.1 us -> 54.1 us (level)
  no operation moved by 1% of the time
where the time goes in v10:
time: 54.1 us; the launch traced here: 53.8 us
  blocking collectives  23.9 us (44%)
  starting transfers between devices  21.2 us (39%)
  Pallas kernels  4.19 us (8%)
  local copies, waits for them, and re-layouts  2.42 us (4%)
  waiting for transfers between devices  2.05 us (4%)
    all_gather x1, blocking collectives, body(): row_side = lax.all_gather(days, 'col', axis=0)  19.4 us
    all_to_all x1, starting transfers between devices, body(): lax.all_to_all(pieces, ('row', 'day'), 0, 0, tiled=True)  11.6 us
    ppermute x1, starting transfers between devices, body(): turned = lax.ppermute(white, AXES, turn)  9.54 us
    all_gather x1, blocking collectives, body(): days = lax.all_gather(white, 'day', axis=0)  4.5 us
    pallas_call x1, Pallas kernels, stack(): pl.pallas_call(stack_kernel, in_specs=[vmem, vmem, vmem], out_specs=vmem,...  4.04 us
    all_to_all x1, waiting for transfers between devices, body(): lax.all_to_all(pieces, ('row', 'day'), 0, 0, tiled=True)  2.05 us
    unnamed x6, local copies, waits for them, and re-layouts  1.42 us
  transfers between devices with their start and end apart: 2, of which 1 were waited for; matrix products, arithmetic and copies ran while one was open for 0% of the time, Pallas kernels for 0%

profile of v10, /device:TPU:4, one launch (start us, length us, event | category | flops | bytes accessed | tf_op | source)
XLA Modules:
  0.0 53.8 jit_solution(7761288078723162889)
XLA Ops:
  0.0 0.0 copy-start.1
  0.0 0.7 %copy-done.1 = bf16[1,6,4,512]{3,2,1,0:T(4,128)(2,1)S(1)} copy-done((bf16[1,6,4,512]{3,2,1,0:T(4,128)(2,1)S(1)}, bf16[1,6,4,512]{3,2,1,0:T(4,128)(2,1)}, u32[]{:S(2)}) %copy-start.1) | copy-done | bytes 24600
  0.7 0.0 copy-start.2
  0.7 0.7 %copy-done.2 = s32[1,6,4]{1,2,0:T(4,128)S(1)} copy-done((s32[1,6,4]{1,2,0:T(4,128)S(1)}, s32[1,6,4]{1,2,0:T(4,128)}, u32[]{:S(2)}) %copy-start.2) | copy-done | bytes 120
  1.4 0.1 whiten.1
  1.6 9.5 %collective-permute-start = (bf16[96,128]{1,0:T(8,128)(2,1)S(1)}, bf16[96,128]{1,0:T(8,128)(2,1)S(1)}, u32[]{:S(2)}, u32[]{:S(2)}) collective-permute-start(bf16[96,128]{1,0:T(8,128)(2,1)S(1)} %whiten.1), channel_id=1, source_target_pairs={{0,320},{1,321},{2,352},{3,353},{4,448},{5,449},{6,288},{7,289},{8... | collective-permute-start | bytes 73736 | tf_op jit(solution)/shard_map/ppermute | solution.py:226
  11.1 4.5 %all-gather = bf16[192,128]{1,0:T(8,128)(2,1)S(1)} all-gather(bf16[96,128]{1,0:T(8,128)(2,1)S(1)} %whiten.1), channel_id=2, replica_groups=mesh['row'=16,'col'=16,'day'=2] {'day'}, dimensions={0}, use_global_device_ids=true | all-gather | bytes 73728 | tf_op jit(solution)/shard_map/all_gather | solution.py:227
  15.6 0.0 collective-permute-done
  15.6 1.0 %broadcast_in_dim.4 = bf16[32,96,128]{2,1,0:T(8,128)(2,1)} broadcast(bf16[96,128]{1,0:T(8,128)(2,1)S(1)} %collective-permute-done), dimensions={1,2} | broadcast | bytes 811008 | tf_op jit(solution)/shard_map/broadcast_in_dim | solution.py:229
  16.6 11.6 %all-to-all-start = ((bf16[32,96,128]{2,1,0:T(8,128)(2,1)}), bf16[32,96,128]{2,1,0:T(8,128)(2,1)S(1)}, u32[]{:S(2)}, u32[]{:S(2)}) async-start(bf16[32,96,128]{2,1,0:T(8,128)(2,1)} %broadcast_in_dim.4), calls=%async_computation | async-start | bytes 1572864 | tf_op jit(solution)/shard_map/all_to_all | solution.py:230
  28.3 0.0 copy-start
  28.3 19.4 %all-gather.1 = bf16[32,96,128]{2,1,0:T(8,128)(2,1)S(1)} all-gather(bf16[2,96,128]{2,1,0:T(8,128)(2,1)S(1)} %bitcast.8), channel_id=3, replica_groups=mesh['row'=16,'col'=16,'day'=2] {'col'}, dimensions={0}, use_global_device_ids=true | all-gather | bytes 835584 | tf_op jit(solution)/shard_map/all_gather | solution.py:231
  47.7 2.1 %all-to-all-done = bf16[32,96,128]{2,1,0:T(8,128)(2,1)S(1)} async-done(((bf16[32,96,128]{2,1,0:T(8,128)(2,1)}), bf16[32,96,128]{2,1,0:T(8,128)(2,1)S(1)}, u32[]{:S(2)}, u32[]{:S(2)}) %all-to-all-start) | async-done | bytes 786464 | tf_op jit(solution)/shard_map/all_to_all | solution.py:230
  49.8 0.0 copy-done
  49.8 4.0 %stack.1 = bf16[32,32,128]{2,1,0:T(8,128)(2,1)} custom-call(bf16[16,2,96,128]{3,2,1,0:T(8,128)(2,1)S(1)} %bitcast.6, bf16[16,2,96,128]{3,2,1,0:T(8,128)(2,1)S(1)} %bitcast.5, bf16[512,256]{1,0:T(8,128)(2,1)S(1)} %copy-done), custom_call_target="tpu_custom_call" | custom-call | tf_op jit(solution)/shard_map/stack/pallas_call | solution.py:203
Async XLA Ops:
  0.0 0.7 %copy-start.1 = (bf16[1,6,4,512]{3,2,1,0:T(4,128)(2,1)S(1)}, bf16[1,6,4,512]{3,2,1,0:T(4,128)(2,1)}, u32[]{:S(2)}) copy-start(bf16[1,6,4,512]{3,2,1,0:T(4,128)(2,1)} %spec_ref.1) | copy-start | bytes 73732
  0.7 0.7 %copy-start.2 = (s32[1,6,4]{1,2,0:T(4,128)S(1)}, s32[1,6,4]{1,2,0:T(4,128)}, u32[]{:S(2)}) copy-start(s32[1,6,4]{1,2,0:T(4,128)} %param.4) | copy-start | bytes 292
  1.6 14.1 %collective-permute-start = (bf16[96,128]{1,0:T(8,128)(2,1)S(1)}, bf16[96,128]{1,0:T(8,128)(2,1)S(1)}, u32[]{:S(2)}, u32[]{:S(2)}) collective-permute-start(bf16[96,128]{1,0:T(8,128)(2,1)S(1)} %whiten.1), channel_id=1, source_target_pairs={{0,320},{1,321},{2,352},{3,353},{4,448},{5,449},{6,288},{7,289},{8... | collective-permute-start | bytes 73736 | tf_op jit(solution)/shard_map/ppermute | solution.py:226
  16.6 33.1 %all-to-all-start = ((bf16[32,96,128]{2,1,0:T(8,128)(2,1)}), bf16[32,96,128]{2,1,0:T(8,128)(2,1)S(1)}, u32[]{:S(2)}, u32[]{:S(2)}) async-start(bf16[32,96,128]{2,1,0:T(8,128)(2,1)} %broadcast_in_dim.4), calls=%async_computation | async-start | bytes 1572864 | tf_op jit(solution)/shard_map/all_to_all | solution.py:230
  28.3 21.5 %copy-start = (bf16[512,256]{1,0:T(8,128)(2,1)S(1)}, bf16[512,256]{1,0:T(8,128)(2,1)}, u32[]{:S(2)}) copy-start(bf16[512,256]{1,0:T(8,128)(2,1)} %constant.2.clone.table_ref) | copy-start | bytes 786436

commit v11 on v10

--- a/solution.py
+++ b/solution.py
@@ -97,7 +97,7 @@
                         v = -v
                     seconds[source, day, h, part] = v.astype(DT)
 
-    @pl.loop(0, 8, unroll=2)
+    @pl.loop(0, 8, unroll=8)
     def _(j):
         holder = held(col_start + j)
         for day in range(2):
@@ -113,7 +113,7 @@
 
     @pl.when(corner)
     def _():
-        @pl.loop(0, 8, unroll=2)
+        @pl.loop(0, 8, unroll=8)
         def _(j):
             for day in range(2):
                 at = pl.ds(pl.multiple_of(day * 192 + j * 24, 8), 24)

time: 54.1 us -> 54.1 us (level)
  no operation moved by 1% of the time
where the time goes in v11:
time: 54.1 us; the launch traced here: 53.7 us
  blocking collectives  23.9 us (44%)
  starting transfers between devices  21.2 us (39%)
  Pallas kernels  4.11 us (8%)
  local copies, waits for them, and re-layouts  2.42 us (4%)
  waiting for transfers between devices  2.05 us (4%)
    all_gather x1, blocking collectives, body(): row_side = lax.all_gather(days, 'col', axis=0)  19.4 us
    all_to_all x1, starting transfers between devices, body(): lax.all_to_all(pieces, ('row', 'day'), 0, 0, tiled=True)  11.6 us
    ppermute x1, starting transfers between devices, body(): turned = lax.ppermute(white, AXES, turn)  9.54 us
    all_gather x1, blocking collectives, body(): days = lax.all_gather(white, 'day', axis=0)  4.5 us
    pallas_call x1, Pallas kernels, stack(): pl.pallas_call(stack_kernel, in_specs=[vmem, vmem, vmem], out_specs=vmem,...  3.96 us
    all_to_all x1, waiting for transfers between devices, body(): lax.all_to_all(pieces, ('row', 'day'), 0, 0, tiled=True)  2.05 us
    unnamed x6, local copies, waits for them, and re-layouts  1.42 us
  transfers between devices with their start and end apart: 2, of which 1 were waited for; matrix products, arithmetic and copies ran while one was open for 0% of the time, Pallas kernels for 0%

profile of v11, /device:TPU:4, one launch (start us, length us, event | category | flops | bytes accessed | tf_op | source)
XLA Modules:
  0.0 53.7 jit_solution(6178765878081445132)
XLA Ops:
  0.0 0.0 copy-start.1
  0.0 0.7 %copy-done.1 = bf16[1,6,4,512]{3,2,1,0:T(4,128)(2,1)S(1)} copy-done((bf16[1,6,4,512]{3,2,1,0:T(4,128)(2,1)S(1)}, bf16[1,6,4,512]{3,2,1,0:T(4,128)(2,1)}, u32[]{:S(2)}) %copy-start.1) | copy-done | bytes 24600
  0.7 0.0 copy-start.2
  0.7 0.7 %copy-done.2 = s32[1,6,4]{1,2,0:T(4,128)S(1)} copy-done((s32[1,6,4]{1,2,0:T(4,128)S(1)}, s32[1,6,4]{1,2,0:T(4,128)}, u32[]{:S(2)}) %copy-start.2) | copy-done | bytes 120
  1.4 0.1 whiten.1
  1.6 9.5 %collective-permute-start = (bf16[96,128]{1,0:T(8,128)(2,1)S(1)}, bf16[96,128]{1,0:T(8,128)(2,1)S(1)}, u32[]{:S(2)}, u32[]{:S(2)}) collective-permute-start(bf16[96,128]{1,0:T(8,128)(2,1)S(1)} %whiten.1), channel_id=1, source_target_pairs={{0,320},{1,321},{2,352},{3,353},{4,448},{5,449},{6,288},{7,289},{8... | collective-permute-start | bytes 73736 | tf_op jit(solution)/shard_map/ppermute | solution.py:226
  11.1 4.5 %all-gather = bf16[192,128]{1,0:T(8,128)(2,1)S(1)} all-gather(bf16[96,128]{1,0:T(8,128)(2,1)S(1)} %whiten.1), channel_id=2, replica_groups=mesh['row'=16,'col'=16,'day'=2] {'day'}, dimensions={0}, use_global_device_ids=true | all-gather | bytes 73728 | tf_op jit(solution)/shard_map/all_gather | solution.py:227
  15.6 0.0 collective-permute-done
  15.6 1.0 %broadcast_in_dim.4 = bf16[32,96,128]{2,1,0:T(8,128)(2,1)} broadcast(bf16[96,128]{1,0:T(8,128)(2,1)S(1)} %collective-permute-done), dimensions={1,2} | broadcast | bytes 811008 | tf_op jit(solution)/shard_map/broadcast_in_dim | solution.py:229
  16.6 11.6 %all-to-all-start = ((bf16[32,96,128]{2,1,0:T(8,128)(2,1)}), bf16[32,96,128]{2,1,0:T(8,128)(2,1)S(1)}, u32[]{:S(2)}, u32[]{:S(2)}) async-start(bf16[32,96,128]{2,1,0:T(8,128)(2,1)} %broadcast_in_dim.4), calls=%async_computation | async-start | bytes 1572864 | tf_op jit(solution)/shard_map/all_to_all | solution.py:230
  28.3 0.0 copy-start
  28.3 19.4 %all-gather.1 = bf16[32,96,128]{2,1,0:T(8,128)(2,1)S(1)} all-gather(bf16[2,96,128]{2,1,0:T(8,128)(2,1)S(1)} %bitcast.8), channel_id=3, replica_groups=mesh['row'=16,'col'=16,'day'=2] {'col'}, dimensions={0}, use_global_device_ids=true | all-gather | bytes 835584 | tf_op jit(solution)/shard_map/all_gather | solution.py:231
  47.7 2.1 %all-to-all-done = bf16[32,96,128]{2,1,0:T(8,128)(2,1)S(1)} async-done(((bf16[32,96,128]{2,1,0:T(8,128)(2,1)}), bf16[32,96,128]{2,1,0:T(8,128)(2,1)S(1)}, u32[]{:S(2)}, u32[]{:S(2)}) %all-to-all-start) | async-done | bytes 786464 | tf_op jit(solution)/shard_map/all_to_all | solution.py:230
  49.8 0.0 copy-done
  49.8 4.0 %stack.1 = bf16[32,32,128]{2,1,0:T(8,128)(2,1)} custom-call(bf16[16,2,96,128]{3,2,1,0:T(8,128)(2,1)S(1)} %bitcast.6, bf16[16,2,96,128]{3,2,1,0:T(8,128)(2,1)S(1)} %bitcast.5, bf16[512,256]{1,0:T(8,128)(2,1)S(1)} %copy-done), custom_call_target="tpu_custom_call" | custom-call | tf_op jit(solution)/shard_map/stack/pallas_call | solution.py:203
Async XLA Ops:
  0.0 0.7 %copy-start.1 = (bf16[1,6,4,512]{3,2,1,0:T(4,128)(2,1)S(1)}, bf16[1,6,4,512]{3,2,1,0:T(4,128)(2,1)}, u32[]{:S(2)}) copy-start(bf16[1,6,4,512]{3,2,1,0:T(4,128)(2,1)} %spec_ref.1) | copy-start | bytes 73732
  0.7 0.7 %copy-start.2 = (s32[1,6,4]{1,2,0:T(4,128)S(1)}, s32[1,6,4]{1,2,0:T(4,128)}, u32[]{:S(2)}) copy-start(s32[1,6,4]{1,2,0:T(4,128)} %param.4) | copy-start | bytes 292
  1.6 14.1 %collective-permute-start = (bf16[96,128]{1,0:T(8,128)(2,1)S(1)}, bf16[96,128]{1,0:T(8,128)(2,1)S(1)}, u32[]{:S(2)}, u32[]{:S(2)}) collective-permute-start(bf16[96,128]{1,0:T(8,128)(2,1)S(1)} %whiten.1), channel_id=1, source_target_pairs={{0,320},{1,321},{2,352},{3,353},{4,448},{5,449},{6,288},{7,289},{8... | collective-permute-start | bytes 73736 | tf_op jit(solution)/shard_map/ppermute | solution.py:226
  16.6 33.1 %all-to-all-start = ((bf16[32,96,128]{2,1,0:T(8,128)(2,1)}), bf16[32,96,128]{2,1,0:T(8,128)(2,1)S(1)}, u32[]{:S(2)}, u32[]{:S(2)}) async-start(bf16[32,96,128]{2,1,0:T(8,128)(2,1)} %broadcast_in_dim.4), calls=%async_computation | async-start | bytes 1572864 | tf_op jit(solution)/shard_map/all_to_all | solution.py:230
  28.3 21.5 %copy-start = (bf16[512,256]{1,0:T(8,128)(2,1)S(1)}, bf16[512,256]{1,0:T(8,128)(2,1)}, u32[]{:S(2)}) copy-start(bf16[512,256]{1,0:T(8,128)(2,1)} %constant.2.clone.table_ref) | copy-start | bytes 786436
